TPU v7x, 256 devices: a whole 4x4x8 slice. The times are simulated.
256 devices in a mesh: blk: 16 (over y_lo, x, core), tm: 16 (over y_hi, z).
Axes of the slice: x: 4, y: 4 (y_hi: 2, y_lo: 2; y = y_hi * 2 + y_lo), z: 8, core: 2. Of those that a mesh axis runs over, the one named last changes fastest.
Arguments:
- rainfall: bfloat16 [10240, 8192], P('blk', 'tm'), as said below
- runoff: bfloat16 [10240, 8192], P('blk', 'tm'), as said below
- lag_days: int32 [1], replicated, may hold values from 0 to 30
Outputs:
- correlation: float32 [10240, 10240], P('blk', 'tm')
Inputs may be any that keep to these rules, and one draw needn't show every extreme that they name: `rainfall`: every cell's precipitation and runoff anomalies both vary from day to day, so that both variances are positive. Every cell's runoff anomalies vary from day to day.
All inputs are finite; a program needn't handle non-finite values.
Results may differ from a plain program's by a relative error of at most 0.0003.
Values may be sent and summed in bfloat16 or wider, within the bound.
A program may use at most 128 MiB of HBM per device.

v0:
```python
import jax
import jax.numpy as jnp
from jax import lax
from jax.sharding import PartitionSpec as P

EDGE = 32


def from_behind(shard, axis, by):
    size = lax.axis_size(axis)
    pairs = [(i, i + by) for i in range(size) if 0 <= i + by < size]
    return lax.ppermute(shard, axis, pairs)


def local(rainfall, runoff, lag_days):
    shift_days = lag_days[0]
    local_days = rainfall.shape[1]
    edge = from_behind(runoff[:, :EDGE], "tm", -1)
    longer = jnp.concatenate([runoff, edge], axis=1)
    moved = lax.dynamic_slice_in_dim(longer, shift_days, local_days, 1)
    total = local_days * lax.axis_size("tm")
    global_day = lax.axis_index("tm") * local_days + jnp.arange(local_days, dtype=jnp.int32)
    valid = global_day < total - shift_days
    rain_used = jnp.where(valid[None, :], rainfall, jnp.zeros_like(rainfall))
    flow_used = jnp.where(valid[None, :], moved, jnp.zeros_like(moved))
    samples = (total - shift_days).astype(jnp.float32)
    gathered = lax.all_gather(flow_used, "blk", axis=0, tiled=True)
    column_count = gathered.shape[0] // lax.axis_size("tm")
    column_start = lax.axis_index("tm") * column_count
    rain_float = rain_used.astype(jnp.float32)
    flow_float = flow_used.astype(jnp.float32)
    rain_sum, rain_square, flow_sum, flow_square = lax.psum(
        (
            jnp.sum(rain_float, axis=1),
            jnp.sum(rain_float * rain_float, axis=1),
            jnp.sum(flow_float, axis=1),
            jnp.sum(flow_float * flow_float, axis=1),
        ),
        "tm",
    )
    every_sum, every_square = (
        lax.all_gather(flow_sum, "blk", axis=0, tiled=True),
        lax.all_gather(flow_square, "blk", axis=0, tiled=True),
    )
    mine_sum = lax.dynamic_slice_in_dim(every_sum, column_start, column_count, 0)
    mine_square = lax.dynamic_slice_in_dim(every_square, column_start, column_count, 0)
    summed = lax.psum_scatter(
        lax.dot_general(
            gathered, rain_used, (((1,), (1,)), ((), ())), preferred_element_type=jnp.float32
        ),
        "tm",
        scatter_dimension=0,
        tiled=True,
    )
    cross = summed.T
    covar = cross - rain_sum[:, None] * mine_sum[None, :] / samples
    rain_var = rain_square - rain_sum * rain_sum / samples
    flow_var = mine_square - mine_sum * mine_sum / samples
    return covar / jnp.sqrt(rain_var[:, None] * flow_var[None, :])


def solution(mesh):
    placed = (P("blk", "tm"), P("blk", "tm"), P())
    return jax.shard_map(
        local, mesh=mesh, in_specs=placed, out_specs=P("blk", "tm"), check_vma=False
    )
```

profile of v0, /device:TPU:104, one launch (start us, length us, event | category | flops | bytes accessed | tf_op | source)
XLA Modules:
  0.0 513.1 jit_solution(4948503385672568692)
XLA Ops:
  6.5 0.0 copy-start
  6.5 0.0 all-gather.4.cloned.1.call-start
  6.5 1.0 slice.3
  7.5 2.0 collective-permute-start
  10.2 6.5 %collective-permute-done = bf16[640,32]{1,0:T(8,128)(2,1)S(1)} collective-permute-done((bf16[640,32]{1,0:T(8,128)(2,1)S(1)}, bf16[640,32]{1,0:T(8,128)(2,1)S(1)}, u32[]{:S(2)}, u32[]{:S(2)}) %collective-permute-start) | collective-permute-done | bytes 40992 | tf_op jit(solution)/shard_map/ppermute | solution.py:12
  16.8 3.1 convert_reduce_fusion.1
  19.8 0.0 all-gather.4.cloned.1.call-update
  19.9 0.0 reduce-scatter.2.cloned.1.call-start
  19.9 65.7 %all-gather.4.cloned.1.call-done = bf16[10240,512]{1,0:T(8,128)(2,1)} async-done(((bf16[640,512]{1,0:T(8,128)(2,1)}), bf16[10240,512]{1,0:T(8,128)(2,1)}) %all-gather.4.cloned.1.call-update) | async-done | bytes 10485776 | tf_op jit(solution)/shard_map/all_gather | solution.py:27
  85.6 0.0 copy-done
  85.6 15.8 %fusion.5 = f32[10240,640]{1,0:T(8,128)} fusion(bf16[10240,512]{1,0:T(8,128)(2,1)} %all-gather.4.cloned.1.call-done, bf16[640,512]{1,0:T(8,128)(2,1)S(1)} %copy-done, pred[512]{0:T(512)(128)(4,1)S(1)} %add_compare_fusion), kind=kOutput, calls=%fused_computation.13 | convolution fusion | flops 6711214080 | bytes 37356032 | tf_op jit(solution)/shard_map/dot_general | solution.py:48
  101.4 0.0 reduce-scatter.2.cloned.1.call-update
  101.4 68.9 %all-reduce = (f32[640]{0:T(1024)S(1)}, f32[640]{0:T(1024)S(1)}, f32[640]{0:T(1024)S(1)}, f32[640]{0:T(1024)S(1)}) all-reduce(f32[640]{0:T(1024)S(1)} %get-tuple-element.16, f32[640]{0:T(1024)S(1)} %get-tuple-element.17, f32[640]{0:T(1024)S(1)} %get-tuple-element.6, ...), channel_id=1, replica_groups=mesh['blk'=16,'tm'=16] {'tm'}, use_global_device_ids=true, to_apply=%region_4.5 | all-reduce | flops 2560 | bytes 20480 | tf_op jit(solution)/shard_map/psum | solution.py:32
  170.4 19.5 %all-gather.1 = f32[16,1,640]{2,1,0:T(1,128)S(1)} all-gather(f32[1,1,640]{2,1,0:T(1,128)S(1)} %reshape.11), channel_id=1, replica_groups=mesh['blk'=16,'tm'=16] {'blk'}, dimensions={0}, use_global_device_ids=true | all-gather | bytes 43520 | tf_op jit(solution)/shard_map/all_gather | solution.py:43
  189.9 16.4 %all-gather = f32[16,1,640]{2,1,0:T(1,128)S(1)} all-gather(f32[1,1,640]{2,1,0:T(1,128)S(1)} %reshape.9), channel_id=1, replica_groups=mesh['blk'=16,'tm'=16] {'blk'}, dimensions={0}, use_global_device_ids=true | all-gather | bytes 43520 | tf_op jit(solution)/shard_map/all_gather | solution.py:42
  206.3 0.1 divide_subtract_fusion
  206.4 296.3 %reduce-scatter.2.cloned.1.call-done = f32[640,640]{1,0:T(8,128)} async-done(((f32[10240,640]{1,0:T(8,128)}), f32[640,640]{1,0:T(8,128)}) %reduce-scatter.2.cloned.1.call-update) | async-done | bytes 1638416 | tf_op jit(solution)/shard_map/reduce_scatter | solution.py:47
  502.7 1.8 fusion
  504.5 1.7 copy.5
  (4 shorter events, 0.0 us)
Async XLA Ops:
  6.5 79.0 %copy-start = (bf16[640,512]{1,0:T(8,128)(2,1)S(1)}, bf16[640,512]{1,0:T(8,128)(2,1)}, u32[]{:S(2)}) copy-start(bf16[640,512]{1,0:T(8,128)(2,1)} %param.3) | copy-start | bytes 1966084
  6.5 79.0 %all-gather.4.cloned.1.call-start = ((), (), s32[]{:S(2)}) async-start(), calls=%async_computation.1 | async-start | bytes 11141120 | tf_op jit(solution)/shard_map/all_gather | solution.py:27
  7.5 9.2 %collective-permute-start = (bf16[640,32]{1,0:T(8,128)(2,1)S(1)}, bf16[640,32]{1,0:T(8,128)(2,1)S(1)}, u32[]{:S(2)}, u32[]{:S(2)}) collective-permute-start(bf16[640,32]{1,0:T(8,128)(2,1)S(1)} %slice.3), channel_id=1, source_target_pairs={{1,0},{2,1},{3,2},{4,3},{5,4},{6,5},{7,6},{8,7},{9,8},{10,9},{11,1... | collective-permute-start | bytes 122888 | tf_op jit(solution)/shard_map/ppermute | solution.py:12
  19.9 482.8 %reduce-scatter.2.cloned.1.call-start = ((), (), s32[]{:S(2)}) async-start(), calls=%async_computation.2 | async-start | bytes 27852800 | tf_op jit(solution)/shard_map/reduce_scatter | solution.py:47
Sparse Core Ops, SparseCore 0:
  20.0 65.5 all-gather.3
  101.5 401.1 reduce-scatter.1
where the time goes:
time: 516 us; the launch traced here: 513 us
  waiting for transfers between devices  369 us (72%)
  blocking collectives  105 us (20%)
  matrix products  15.8 us (3%)
  between operations  14.1 us (3%)
    reduce_scatter x1, waiting for transfers between devices, local(): lax.psum_scatter(lax.dot_general(gathered, rain_used, (((1,), (1,)), ((),...  296 us
    psum x1, blocking collectives, local(): lax.psum((jnp.sum(rain_float, axis=1), jnp.sum(rain_float * rain_float, a...  68.9 us
    all_gather x1, waiting for transfers between devices, local(): gathered = lax.all_gather(flow_used, 'blk', axis=0, tiled=True)  65.7 us
    all_gather x1, blocking collectives, local(): lax.all_gather(flow_square, 'blk', axis=0, tiled=True)  19.5 us
    all_gather x1, blocking collectives, local(): lax.all_gather(flow_sum, 'blk', axis=0, tiled=True)  16.4 us
    dot_general x1, matrix products, local(): lax.dot_general(gathered, rain_used, (((1,), (1,)), ((), ())), preferred_...  15.8 us
  transfers between devices with their start and end apart: 3, of which 3 were waited for; matrix products, arithmetic and copies ran while one was open for 0% of the time, Pallas kernels for 0%

commit v1 on v0

v1 whole, which is shorter than its diff:
```python
import jax
import jax.numpy as jnp
from jax import lax
from jax.experimental import pallas as pl
from jax.experimental.pallas import tpu as pltpu
from jax.sharding import PartitionSpec as P

XS, ZS, LANES = 4, 8, 128
ORDER = (0, 1, 3, 2)
WAVES = ((0, 1), (2, 3))


def kernel(
    lag_ref, rain_ref, flow_ref, cross_ref, stat_ref,
    flow_v, rain_v, stage, rain_all, flow_all, acc, relay, final,
    rain_part, flow_part, stat_send, stat_recv,
    load_sem, s1, r1, s2, r2, s3, r3, sx, rx, sc, rc, sr, rr, se, re, sg, rg, sf, rf, st, rt,
):
    rows, days = rain_v.shape
    piece = rows // XS
    strip = rows // 4
    lag = lag_ref[0]
    blk, tm = lax.axis_index("blk"), lax.axis_index("tm")
    yl, x, c = lax.div(blk, 8), lax.rem(lax.div(blk, 2), 4), lax.rem(blk, 2)
    yh, z = lax.div(tm, 8), lax.rem(tm, 8)
    zp, zo = lax.div(z, 2), lax.rem(z, 2)
    other = 1 - yh

    def dev(yl_=None, x_=None, c_=None, yh_=None, z_=None):
        b = (yl if yl_ is None else yl_) * 8 + (x if x_ is None else x_) * 2 + (c if c_ is None else c_)
        t = (yh if yh_ is None else yh_) * 8 + (z if z_ is None else z_)
        return (b, t)

    def xo(d):
        return lax.rem(x + d, XS)

    def zo_(d):
        return lax.rem(z + d + ZS, ZS)

    y = 2 * yh + yl
    yu, yd = lax.rem(y + 1, 4), lax.rem(y + 3, 4)
    up = dev(yl_=lax.rem(yu, 2), yh_=lax.div(yu, 2))
    down = dev(yl_=lax.rem(yd, 2), yh_=lax.div(yd, 2))
    near = dev(yl_=1 - yl)
    sibling = dev(c_=1 - c)
    far = dev(yh_=other)
    far_sibling = dev(yh_=other, c_=1 - c)
    right, left = dev(x_=xo(1)), dev(x_=xo(3))
    ahead, behind = dev(z_=zo_(1)), dev(z_=zo_(-1))

    def swap_pair(k):
        return lax.rem(zp + k, 4)

    def swap_dev(k):
        return dev(z_=2 * swap_pair(k) + c, c_=zo)

    def rcopy(src, dst, send, recv, to):
        return pltpu.make_async_remote_copy(
            src_ref=src, dst_ref=dst, send_sem=send, recv_sem=recv,
            device_id=to, device_id_type=pl.DeviceIdType.MESH,
        )

    pending = []

    def send(copy, when=None):
        if when is None:
            copy.start()
        else:
            pl.when(when)(copy.start)
        pending.append((copy, when))

    load_flow = pltpu.make_async_copy(flow_ref, flow_v, load_sem.at[0])
    load_rain = pltpu.make_async_copy(rain_ref, rain_v, load_sem.at[1])
    load_flow.start()
    load_rain.start()

    crossed = c != zo
    barrier = pltpu.get_barrier_semaphore()
    partners = [dev(x_=xo(d)) for d in (1, 2, 3)]
    partners += [ahead, behind, up, down, far, far_sibling, sibling]
    partners += [swap_dev(k) for k in (1, 2, 3)]

    def greet(to):
        pl.semaphore_signal(barrier, inc=1, device_id=to, device_id_type=pl.DeviceIdType.MESH)

    for to in partners:
        greet(to)

    @pl.when(crossed)
    def _():
        greet(swap_dev(0))

    pl.semaphore_wait(barrier, len(partners) + jnp.where(crossed, 1, 0))

    def part(ref, i):
        return ref.at[pl.ds(pl.multiple_of(i * piece, piece), piece), :]

    def cell(zd, half, col):
        return flow_all.at[zd, half, pl.ds(pl.multiple_of(col * piece, piece), piece), :]

    load_flow.wait()
    own = pltpu.make_async_copy(part(flow_v, x), stage.at[0], r1.at[0])
    own.start()
    for d in (1, 3, 2):
        send(rcopy(part(flow_v, xo(d)), stage.at[d], s1.at[d], r1.at[d], dev(x_=xo(d))))

    load_rain.wait()
    i0 = lax.broadcasted_iota(jnp.int32, (2 * LANES, LANES), 0)
    i1 = lax.broadcasted_iota(jnp.int32, (2 * LANES, LANES), 1)
    shift = jnp.where(i0 == i1 + LANES - lag, 1.0, 0.0).astype(jnp.bfloat16)
    tiles = days // LANES
    for j in range(tiles):
        p = (j + tiles - 1) % tiles
        two = jnp.concatenate(
            [rain_v[:, p * LANES:(p + 1) * LANES], rain_v[:, j * LANES:(j + 1) * LANES]], axis=1
        )
        rain_all[z + 1, :, j * LANES:(j + 1) * LANES] = jnp.dot(
            two, shift, preferred_element_type=jnp.float32
        ).astype(jnp.bfloat16)

    def strip_of(chunk, q):
        return rain_all.at[chunk + 1, q * strip:(q + 1) * strip, :]

    edges = [
        rcopy(
            rain_all.at[ZS, q * strip:(q + 1) * strip, 0:LANES],
            rain_all.at[0, q * strip:(q + 1) * strip, 0:LANES],
            se.at[q], re.at[q], far,
        )
        for q in range(4)
    ]

    @pl.when(yh == 0)
    def _():
        rain_all[0, :, 0:LANES] = jnp.zeros((rows, LANES), jnp.bfloat16)

    def pass_edge(chunk, q):
        pl.when((chunk == ZS - 1) & (yh == 0))(edges[q].start)

    def ring_copy(way, q, s):
        chunk = zo_(1 - s) if way == 0 else zo_(s - 1)
        at = strip_of(chunk, q)
        return rcopy(at, at, sr.at[way, q, s - 1], rr.at[way, q, s - 1], ahead if way == 0 else behind)

    def reach(way, q):
        return 4 if (q + way) % 2 == 0 else 3

    def ring_start(q):
        pass_edge(z, q)
        for way in (0, 1):
            send(ring_copy(way, q, 1))

    def ring_arrive(way, q, s):
        chunk = zo_(-s) if way == 0 else zo_(s)
        at = strip_of(chunk, q)
        rcopy(at, at, sr.at[way, q, s - 1], rr.at[way, q, s - 1], behind).wait_recv()
        if s < reach(way, q):
            send(ring_copy(way, q, s + 1))
        pass_edge(chunk, q)

    for q in WAVES[0]:
        ring_start(q)

    for k in ORDER:
        d = lax.rem(x - swap_pair(k) + XS, XS)
        src = stage.at[d]
        rcopy(src, src, s1.at[0], r1.at[d], right).wait_recv()
        dst = cell(z, yl, x)
        remote = rcopy(src, dst, s2.at[k], r2.at[k], swap_dev(k))
        if k == 0:
            send(remote, crossed)
            pl.when(jnp.logical_not(crossed))(pltpu.make_async_copy(src, dst, r2.at[0]).start)
        else:
            send(remote)

    def home(k):
        return 2 * lax.rem(zp - k + 4, 4) + c

    first = yl == other

    def to_sibling(at, j, o):
        send(rcopy(at, at, sc.at[j, o], rc.at[j, o], sibling))

    def along_x(at, j, when=None):
        send(rcopy(at, at, sx.at[0, j], rx.at[0, j], right), when)
        send(rcopy(at, at, sx.at[1, j], rx.at[1, j], left), when)

    def half_of(j):
        return other if j < 4 else yh

    def arrive_own(i):
        k = ORDER[i]
        at = cell(home(k), yl, x)
        rcopy(at, at, s2.at[k], r2.at[k], right).wait_recv()
        send(rcopy(at, at, s3.at[k], r3.at[k], near))
        along_x(at, i, first)
        to_sibling(at, jnp.where(first, i, i + 4), 0)

    def arrive_near(i):
        k = ORDER[i]
        at = cell(home(k), 1 - yl, x)
        rcopy(at, at, s3.at[k], r3.at[k], near).wait_recv()
        j = jnp.where(first, i + 4, i)
        along_x(at, j)
        to_sibling(at, j, 0)

    def late_own(i):
        along_x(cell(home(ORDER[i]), yl, x), i + 4, jnp.logical_not(first))

    def arrive_x(j, o):
        at = cell(home(ORDER[j % 4]), half_of(j), xo({1: 3, 2: 1, 3: 2}[o]))
        rcopy(at, at, sx.at[o - 1, j], rx.at[o - 1, j], right).wait_recv()
        if o == 1 and j % 2 == 0:
            send(rcopy(at, at, sx.at[2, j], rx.at[2, j], right))
        if o == 2 and j % 2 == 1:
            send(rcopy(at, at, sx.at[2, j], rx.at[2, j], left))
        to_sibling(at, j, o)

    def flow_ready(h):
        for j in range(4 * h, 4 * h + 4):
            zd = 2 * lax.rem(zp - ORDER[j % 4] + 4, 4) + (1 - c)
            for o in range(4):
                at = cell(zd, half_of(j), xo((0, 3, 1, 2)[o]))
                rcopy(at, at, sc.at[j, o], rc.at[j, o], sibling).wait_recv()

    lane = lax.broadcasted_iota(jnp.int32, (strip, LANES), 1)

    def folded(v):
        return sum(v[:, t * LANES:(t + 1) * LANES] for t in range(tiles))

    def multiply(q, h):
        at = slice(q * strip, (q + 1) * strip)
        half = other if h == 0 else yh
        acc[h, at, :] = jnp.zeros((strip, rows), jnp.float32)

        def step(zd, carry):
            before = rain_all[zd, at, 0:LANES].astype(jnp.float32)
            here = rain_all[zd + 1, at, 0:LANES].astype(jnp.float32)
            head = jnp.where(lane < lag, before, here).astype(jnp.bfloat16)
            used = jnp.concatenate([head, rain_all[zd + 1, at, LANES:]], axis=1)
            acc[h, at, :] += lax.dot_general(
                used, flow_all[zd, half], (((1,), (1,)), ((), ())), preferred_element_type=jnp.float32
            )
            if h == 0:
                wide = used.astype(jnp.float32)
                rain_part[0, at, :] += folded(wide)
                rain_part[1, at, :] += folded(wide * wide)
            return carry

        lax.fori_loop(0, ZS, step, 0)

    def flow_stats(h):
        half = other if h == 0 else yh
        blocks = rows // LANES
        flow_part[h] = jnp.zeros((2, rows, LANES), jnp.float32)
        lanes = lax.broadcasted_iota(jnp.int32, (LANES, LANES), 1)

        def step(i, carry):
            zd = 2 * lax.div(i, blocks) + c
            at = pl.ds(pl.multiple_of(lax.rem(i, blocks) * LANES, LANES), LANES)
            wide = flow_all[zd, half, at, :].astype(jnp.float32)
            skip = jnp.where((yh == 0) & (zd == 0), lag, 0)
            head = jnp.where(lanes < skip, 0.0, wide[:, 0:LANES])
            wide = jnp.concatenate([head, wide[:, LANES:]], axis=1)
            flow_part[h, 0, at, :] += folded(wide)
            flow_part[h, 1, at, :] += folded(wide * wide)
            return carry

        lax.fori_loop(0, 4 * blocks, step, 0)

    def rows_of(ref, b):
        return jnp.sum(ref[b * LANES:(b + 1) * LANES, :].T, axis=0, keepdims=True)

    def share_stats():
        for b in range(rows // LANES):
            rs, rq = rows_of(rain_part.at[0], b), rows_of(rain_part.at[1], b)
            zero = jnp.zeros((4, LANES), jnp.float32)
            for i, h in ((0, 1), (1, 0)):
                fs, fq = rows_of(flow_part.at[h, 0], b), rows_of(flow_part.at[h, 1], b)
                stat_send[i, :, b * LANES:(b + 1) * LANES] = jnp.concatenate([fs, fq, rs, rq, zero], axis=0)
        for i, (src, to) in enumerate(((0, sibling), (1, far), (1, far_sibling))):
            send(rcopy(stat_send.at[src], stat_recv.at[i], st.at[i], rt.at[i], to))

    def take_stats():
        for i in range(3):
            at = stat_recv.at[i]
            rcopy(at, at, st.at[i], rt.at[i], sibling).wait_recv()
        is_flow = lax.broadcasted_iota(jnp.int32, (8, rows), 0) < 2
        halves = stat_recv[0] + stat_recv[2]
        stat_ref[...] = stat_send[0] + stat_recv[1] + jnp.where(is_flow, halves, 0.0)

    def strip_at(ref, q):
        return ref.at[q * strip:(q + 1) * strip, :]

    def give(q):
        send(rcopy(strip_at(acc.at[0], q), strip_at(relay, q), sg.at[q], rg.at[q], up if q % 2 == 0 else down))

    def hand_on(q):
        at = strip_at(relay, q)
        rcopy(at, at, sg.at[q], rg.at[q], up).wait_recv()
        send(rcopy(at, strip_at(final, q), sf.at[q], rf.at[q], up if q % 2 == 0 else down))

    def finish(q):
        at = slice(q * strip, (q + 1) * strip)
        ref = strip_at(final, q)
        rcopy(ref, ref, sf.at[q], rf.at[q], up).wait_recv()
        cross_ref[at, :] = acc[1, at, :] + final[at, :]

    def edge_ready(q):
        pl.when(yh == 1)(edges[q].wait_recv)

    events = []

    def at_time(t, *calls):
        events.append((t, len(events), calls))

    for i in range(4):
        at_time(9 + 3.3 * i, lambda i=i: arrive_own(i))
        at_time(13 + 3.3 * i, lambda i=i: arrive_near(i))
        at_time(26.5 + 0.1 * i, lambda i=i: late_own(i))
    for j in range(8):
        at_time(16.5 + 4.9 * j, lambda j=j: arrive_x(j, 1), lambda j=j: arrive_x(j, 2))
        at_time(23.5 + 4.9 * j, lambda j=j: arrive_x(j, 3))
    for w, wave in enumerate(WAVES):
        n = 0
        for s in (1, 2, 3, 4):
            for q in wave:
                for way in (0, 1):
                    if s <= reach(way, q):
                        at_time(8 + 3.8 * (7 * w + n), lambda way=way, q=q, s=s: ring_arrive(way, q, s))
                n += 1 if s < 4 else 0.5
                if w + 1 < len(WAVES) and s == 3:
                    at_time(8 + 3.8 * (7 * w + n) - 3, lambda q=WAVES[w + 1][wave.index(q)]: ring_start(q))

    def send_half(wave):
        for q in wave:
            edge_ready(q)
            multiply(q, 0)
            give(q)

    rain_part[...] = jnp.zeros(rain_part.shape, jnp.float32)
    at_time(44, lambda: flow_ready(0), lambda: send_half(WAVES[0]))
    at_time(46, lambda: flow_stats(0))
    at_time(54, *[lambda q=q: hand_on(q) for q in WAVES[0]])
    at_time(100, lambda: send_half(WAVES[1]))
    at_time(101, lambda: flow_ready(1), lambda: flow_stats(1), share_stats)
    at_time(102, *[lambda q=q: multiply(q, 1) for q in WAVES[0]])
    at_time(103, *[lambda q=q: hand_on(q) for q in WAVES[1]])
    at_time(104, *[lambda q=q: multiply(q, 1) for q in WAVES[1]])
    at_time(105, take_stats)
    at_time(106, *[lambda q=q: finish(q) for q in range(4)])

    for _, _, calls in sorted(events, key=lambda e: e[:2]):
        for call in calls:
            call()

    for copy, when in pending:
        if when is None:
            copy.wait_send()
        else:
            pl.when(when)(copy.wait_send)
    for q in range(4):
        pl.when(yh == 0)(edges[q].wait_send)


def local(rainfall, runoff, lag_days):
    rows, days = rainfall.shape
    dma = pltpu.SemaphoreType.DMA
    bf16, f32 = jnp.bfloat16, jnp.float32
    cross, stats = pl.pallas_call(
        kernel,
        out_shape=(jax.ShapeDtypeStruct((rows, rows), f32), jax.ShapeDtypeStruct((8, rows), f32)),
        in_specs=[
            pl.BlockSpec(memory_space=pltpu.SMEM),
            pl.BlockSpec(memory_space=pl.ANY),
            pl.BlockSpec(memory_space=pl.ANY),
        ],
        out_specs=[pl.BlockSpec(memory_space=pltpu.VMEM)] * 2,
        scratch_shapes=[
            pltpu.VMEM((rows, days), bf16),
            pltpu.VMEM((rows, days), bf16),
            pltpu.VMEM((XS, rows // XS, days), bf16),
            pltpu.VMEM((ZS + 1, rows, days), bf16),
            pltpu.VMEM((ZS, 2, rows, days), bf16),
            pltpu.VMEM((2, rows, rows), f32),
            pltpu.VMEM((rows, rows), f32),
            pltpu.VMEM((rows, rows), f32),
            pltpu.VMEM((2, rows, LANES), f32),
            pltpu.VMEM((2, 2, rows, LANES), f32),
            pltpu.VMEM((2, 8, rows), f32),
            pltpu.VMEM((3, 8, rows), f32),
            dma((2,)),
            dma((4,)), dma((4,)),
            dma((4,)), dma((4,)),
            dma((4,)), dma((4,)),
            dma((3, 8)), dma((3, 8)),
            dma((8, 4)), dma((8, 4)),
            dma((2, 4, 4)), dma((2, 4, 4)),
            dma((4,)), dma((4,)),
            dma((4,)), dma((4,)),
            dma((4,)), dma((4,)),
            dma((3,)), dma((3,)),
        ],
        compiler_params=pltpu.CompilerParams(
            collective_id=0, has_side_effects=True, vmem_limit_bytes=48 * 2**20
        ),
        cost_estimate=pl.CostEstimate(
            flops=2 * rows * 2 * rows * ZS * days, bytes_accessed=4 * rows * rows, transcendentals=0
        ),
    )(lag_days, rainfall, runoff)
    total = days * lax.axis_size("tm")
    samples = (total - lag_days[0]).astype(f32)
    flow_sum, flow_square, rain_sum, rain_square = stats[0], stats[1], stats[2], stats[3]
    covar = cross - rain_sum[:, None] * flow_sum[None, :] / samples
    rain_var = rain_square - rain_sum * rain_sum / samples
    flow_var = flow_square - flow_sum * flow_sum / samples
    return covar / jnp.sqrt(rain_var[:, None] * flow_var[None, :])


def solution(mesh):
    placed = (P("blk", "tm"), P("blk", "tm"), P())
    return jax.shard_map(
        local, mesh=mesh, in_specs=placed, out_specs=P("blk", "tm"), check_vma=False
    )
```

time: 516 us -> 131 us (0.25)
  waiting for transfers between devices: 369 us -> 0 us
  Pallas kernels: 0 us -> 126 us
  blocking collectives: 105 us -> 0 us
  matrix products: 15.8 us -> 0 us
  between operations: 14.1 us -> 0.69 us
    reduce_scatter x1 -> x0, waiting for transfers between devices: 296 us -> none  [local(): lax.psum_scatter(lax.dot_general(gathered, rain_used, (((1,), (1,)), ((),...]
    pallas_call x0 -> x1, Pallas kernels: none -> 126 us  [local(): pl.pallas_call(kernel, out_shape=(jax.ShapeDtypeStruct((rows, rows), f32)...]
    psum x1 -> x0, blocking collectives: 68.9 us -> none  [local(): lax.psum((jnp.sum(rain_float, axis=1), jnp.sum(rain_float * rain_float, a...]
    all_gather x1 -> x0, waiting for transfers between devices: 65.7 us -> none  [local(): gathered = lax.all_gather(flow_used, 'blk', axis=0, tiled=True)]
    all_gather x2 -> x0, blocking collectives: 36 us -> none  [the longest x1 19.5 us: local(): lax.all_gather(flow_square, 'blk', axis=0, tiled=True)]
    dot_general x1 -> x0, matrix products: 15.8 us -> none  [local(): lax.dot_general(gathered, rain_used, (((1,), (1,)), ((), ())), preferred_...]
    ppermute x1 -> x0, waiting for transfers between devices: 6.53 us -> none  [from_behind(): return lax.ppermute(shard, axis, pairs)]
  transfers between devices with their start and end apart: 3 -> 0, of which waited for: 3 -> 0; matrix products, arithmetic and copies ran while one was open for 0% -> 0% of each run, Pallas kernels for 0% -> 0%
where the time goes in v1:
time: 131 us
  Pallas kernels  126 us (96%)
  local copies, waits for them, and re-layouts  2.17 us (2%)
  other arithmetic  1.61 us (1%)
    pallas_call x1, Pallas kernels, local(): pl.pallas_call(kernel, out_shape=(jax.ShapeDtypeStruct((rows, rows), f32)...  126 us

profile of v1, /device:TPU:104, one launch (start us, length us, event | category | flops | bytes accessed | tf_op | source)
XLA Modules:
  0.0 130.9 jit_solution(3302344467322181310)
XLA Ops:
  0.7 0.0 copy-start
  0.7 1.1 copy-done
  1.7 0.0 copy-start.1
  1.7 1.1 copy-done.1
  2.8 126.5 %shard_map.37 = (f32[640,640]{1,0:T(8,128)S(1)}, f32[8,640]{1,0:T(8,128)S(1)}) custom-call(s32[1]{0:T(128)S(6)} %copy.4.lag_ref, bf16[640,512]{1,0:T(8,128)(2,1)S(1)} %copy-done, bf16[640,512]{1,0:T(8,128)(2,1)S(1)} %copy-done.1), custom_call_target="tpu_custom_call" | custom-call | flops 6710886400 | bytes 1638400 | tf_op jit(solution)/shard_map/pallas_call | solution.py:370
  129.3 1.6 %rsqrt_multiply_fusion = f32[640,640]{1,0:T(8,128)} fusion(f32[640,640]{1,0:T(8,128)S(1)} %get-tuple-element.7, f32[640]{0:T(1024)S(1)} %get-tuple-element.10, f32[640]{0:T(1024)S(1)} %divide_subtract_fusion, f32[]{:T(128)} %bitcast, f32[640]{0:T(1024)S(1)} %get-tuple-element.9, f32[640]{0:T(1024)S(1)} %get-tuple-element.12), kind=kLoop, calls=%fused_computation | loop fusion | flops 2048000 | bytes 3287044 | tf_op jit(solution)/shard_map/div | solution.py:417
  (2 shorter events, 0.0 us)
Async XLA Ops:
  0.7 1.1 copy-start
  1.7 1.1 copy-start.1

commit v2 on v1

--- a/solution.py
+++ b/solution.py
@@ -7,7 +7,9 @@
 
 XS, ZS, LANES = 4, 8, 128
 ORDER = (0, 1, 3, 2)
-WAVES = ((0, 1), (2, 3))
+WAVES = ((0, 1), (2, 3), (4, 5))
+BOUNDS = (0, 160, 320, 416, 512, 576, 640)
+STRIPS = len(BOUNDS) - 1
 
 
 def kernel(
@@ -18,7 +20,7 @@
 ):
     rows, days = rain_v.shape
     piece = rows // XS
-    strip = rows // 4
+    assert rows == BOUNDS[-1]
     lag = lag_ref[0]
     blk, tm = lax.axis_index("blk"), lax.axis_index("tm")
     yl, x, c = lax.div(blk, 8), lax.rem(lax.div(blk, 2), 4), lax.rem(blk, 2)
@@ -119,15 +121,15 @@
         ).astype(jnp.bfloat16)
 
     def strip_of(chunk, q):
-        return rain_all.at[chunk + 1, q * strip:(q + 1) * strip, :]
+        return rain_all.at[chunk + 1, BOUNDS[q]:BOUNDS[q + 1], :]
 
     edges = [
         rcopy(
-            rain_all.at[ZS, q * strip:(q + 1) * strip, 0:LANES],
-            rain_all.at[0, q * strip:(q + 1) * strip, 0:LANES],
+            rain_all.at[ZS, BOUNDS[q]:BOUNDS[q + 1], 0:LANES],
+            rain_all.at[0, BOUNDS[q]:BOUNDS[q + 1], 0:LANES],
             se.at[q], re.at[q], far,
         )
-        for q in range(4)
+        for q in range(STRIPS)
     ]
 
     @pl.when(yh == 0)
@@ -158,8 +160,7 @@
             send(ring_copy(way, q, s + 1))
         pass_edge(chunk, q)
 
-    for q in WAVES[0]:
-        ring_start(q)
+    ring_start(WAVES[0][0])
 
     for k in ORDER:
         d = lax.rem(x - swap_pair(k) + XS, XS)
@@ -173,6 +174,8 @@
         else:
             send(remote)
 
+    ring_start(WAVES[0][1])
+
     def home(k):
         return 2 * lax.rem(zp - k + 4, 4) + c
 
@@ -223,41 +226,42 @@
                 at = cell(zd, half_of(j), xo((0, 3, 1, 2)[o]))
                 rcopy(at, at, sc.at[j, o], rc.at[j, o], sibling).wait_recv()
 
-    lane = lax.broadcasted_iota(jnp.int32, (strip, LANES), 1)
-
     def folded(v):
         return sum(v[:, t * LANES:(t + 1) * LANES] for t in range(tiles))
 
-    def multiply(q, h):
-        at = slice(q * strip, (q + 1) * strip)
+    def multiply(lo, hi, h, s, start):
+        at = slice(lo, hi)
         half = other if h == 0 else yh
-        acc[h, at, :] = jnp.zeros((strip, rows), jnp.float32)
-
-        def step(zd, carry):
+        lane = lax.broadcasted_iota(jnp.int32, (hi - lo, LANES), 1)
+        used = []
+        chunks = (zo_(s), zo_(1 - s))
+        for zd in chunks:
             before = rain_all[zd, at, 0:LANES].astype(jnp.float32)
             here = rain_all[zd + 1, at, 0:LANES].astype(jnp.float32)
             head = jnp.where(lane < lag, before, here).astype(jnp.bfloat16)
-            used = jnp.concatenate([head, rain_all[zd + 1, at, LANES:]], axis=1)
-            acc[h, at, :] += lax.dot_general(
-                used, flow_all[zd, half], (((1,), (1,)), ((), ())), preferred_element_type=jnp.float32
-            )
-            if h == 0:
-                wide = used.astype(jnp.float32)
-                rain_part[0, at, :] += folded(wide)
-                rain_part[1, at, :] += folded(wide * wide)
-            return carry
-
-        lax.fori_loop(0, ZS, step, 0)
-
-    def flow_stats(h):
+            used.append(jnp.concatenate([head, rain_all[zd + 1, at, LANES:]], axis=1))
+        product = lax.dot_general(
+            jnp.concatenate(used, axis=1),
+            jnp.concatenate([flow_all[zd, half] for zd in chunks], axis=1),
+            (((1,), (1,)), ((), ())), preferred_element_type=jnp.float32,
+        )
+        if start:
+            acc[h, at, :] = product
+        else:
+            acc[h, at, :] += product
+        if h == 0:
+            wide = [u.astype(jnp.float32) for u in used]
+            rain_part[0, at, :] += sum(folded(u) for u in wide)
+            rain_part[1, at, :] += sum(folded(u * u) for u in wide)
+
+    def flow_stats(h, m):
         half = other if h == 0 else yh
         blocks = rows // LANES
-        flow_part[h] = jnp.zeros((2, rows, LANES), jnp.float32)
         lanes = lax.broadcasted_iota(jnp.int32, (LANES, LANES), 1)
 
         def step(i, carry):
-            zd = 2 * lax.div(i, blocks) + c
-            at = pl.ds(pl.multiple_of(lax.rem(i, blocks) * LANES, LANES), LANES)
+            zd = 2 * m + c
+            at = pl.ds(pl.multiple_of(i * LANES, LANES), LANES)
             wide = flow_all[zd, half, at, :].astype(jnp.float32)
             skip = jnp.where((yh == 0) & (zd == 0), lag, 0)
             head = jnp.where(lanes < skip, 0.0, wide[:, 0:LANES])
@@ -266,7 +270,7 @@
             flow_part[h, 1, at, :] += folded(wide * wide)
             return carry
 
-        lax.fori_loop(0, 4 * blocks, step, 0)
+        lax.fori_loop(0, blocks, step, 0)
 
     def rows_of(ref, b):
         return jnp.sum(ref[b * LANES:(b + 1) * LANES, :].T, axis=0, keepdims=True)
@@ -290,7 +294,7 @@
         stat_ref[...] = stat_send[0] + stat_recv[1] + jnp.where(is_flow, halves, 0.0)
 
     def strip_at(ref, q):
-        return ref.at[q * strip:(q + 1) * strip, :]
+        return ref.at[BOUNDS[q]:BOUNDS[q + 1], :]
 
     def give(q):
         send(rcopy(strip_at(acc.at[0], q), strip_at(relay, q), sg.at[q], rg.at[q], up if q % 2 == 0 else down))
@@ -301,13 +305,18 @@
         send(rcopy(at, strip_at(final, q), sf.at[q], rf.at[q], up if q % 2 == 0 else down))
 
     def finish(q):
-        at = slice(q * strip, (q + 1) * strip)
+        at = slice(BOUNDS[q], BOUNDS[q + 1])
         ref = strip_at(final, q)
         rcopy(ref, ref, sf.at[q], rf.at[q], up).wait_recv()
         cross_ref[at, :] = acc[1, at, :] + final[at, :]
 
-    def edge_ready(q):
-        pl.when(yh == 1)(edges[q].wait_recv)
+    def edge_ready(wave, s):
+        for zd in (zo_(s), zo_(1 - s)):
+
+            @pl.when((zd == 0) & (yh == 1))
+            def _():
+                for q in wave:
+                    edges[q].wait_recv()
 
     events = []
 
@@ -320,35 +329,55 @@
         at_time(26.5 + 0.1 * i, lambda i=i: late_own(i))
     for j in range(8):
         at_time(16.5 + 4.9 * j, lambda j=j: arrive_x(j, 1), lambda j=j: arrive_x(j, 2))
-        at_time(23.5 + 4.9 * j, lambda j=j: arrive_x(j, 3))
+        at_time(22.5 + 4.9 * j, lambda j=j: arrive_x(j, 3))
+
+    def give_half(w, s):
+        wave = WAVES[w]
+        lo, hi = BOUNDS[wave[0]], BOUNDS[wave[1] + 1]
+        edge_ready(wave, s)
+        multiply(lo, hi, 0, s, s == 1)
+        if s == 4:
+            for q in wave:
+                give(q)
+
+    ring_from, ring_gap = (10, 43, 57.5), (5, 2.1, 1.4)
     for w, wave in enumerate(WAVES):
         n = 0
         for s in (1, 2, 3, 4):
             for q in wave:
                 for way in (0, 1):
                     if s <= reach(way, q):
-                        at_time(8 + 3.8 * (7 * w + n), lambda way=way, q=q, s=s: ring_arrive(way, q, s))
+                        at_time(ring_from[w] + ring_gap[w] * n, lambda way=way, q=q, s=s: ring_arrive(way, q, s))
                 n += 1 if s < 4 else 0.5
                 if w + 1 < len(WAVES) and s == 3:
-                    at_time(8 + 3.8 * (7 * w + n) - 3, lambda q=WAVES[w + 1][wave.index(q)]: ring_start(q))
-
-    def send_half(wave):
-        for q in wave:
-            edge_ready(q)
-            multiply(q, 0)
-            give(q)
+                    at_time(
+                        ring_from[w] + ring_gap[w] * (n - 0.9), lambda q=WAVES[w + 1][wave.index(q)]: ring_start(q)
+                    )
+            if w > 0:
+                at_time(ring_from[w] + ring_gap[w] * (n - 0.5), lambda w=w, s=s: give_half(w, s))
 
     rain_part[...] = jnp.zeros(rain_part.shape, jnp.float32)
-    at_time(44, lambda: flow_ready(0), lambda: send_half(WAVES[0]))
-    at_time(46, lambda: flow_stats(0))
-    at_time(54, *[lambda q=q: hand_on(q) for q in WAVES[0]])
-    at_time(100, lambda: send_half(WAVES[1]))
-    at_time(101, lambda: flow_ready(1), lambda: flow_stats(1), share_stats)
-    at_time(102, *[lambda q=q: multiply(q, 1) for q in WAVES[0]])
-    at_time(103, *[lambda q=q: hand_on(q) for q in WAVES[1]])
-    at_time(104, *[lambda q=q: multiply(q, 1) for q in WAVES[1]])
-    at_time(105, take_stats)
-    at_time(106, *[lambda q=q: finish(q) for q in range(4)])
+    flow_part[...] = jnp.zeros(flow_part.shape, jnp.float32)
+    at_time(39.5, lambda: flow_ready(0))
+    for s in (1, 2, 3, 4):
+        at_time(39 + 2 * s, lambda s=s: give_half(0, s))
+    for m in range(4):
+        at_time(49 + 2 * m, lambda m=m: flow_stats(0, m))
+    at_time(57, *[lambda q=q: hand_on(q) for q in WAVES[0]])
+    at_time(65.5, *[lambda q=q: hand_on(q) for q in WAVES[1]])
+    at_time(101, lambda: flow_ready(1))
+    for m in range(4):
+        at_time(102, lambda m=m: flow_stats(1, m))
+    at_time(103, share_stats)
+    cut = BOUNDS[WAVES[1][0]]
+    for s in (1, 2, 3, 4):
+        at_time(104, lambda s=s: multiply(0, cut, 1, s, s == 1))
+    at_time(105, *[lambda q=q: hand_on(q) for q in WAVES[2]])
+    at_time(106, *[lambda q=q: finish(q) for q in WAVES[0]])
+    for s in (1, 2, 3, 4):
+        at_time(107, lambda s=s: multiply(cut, rows, 1, s, s == 1))
+    at_time(108, *[lambda q=q: finish(q) for q in WAVES[1] + WAVES[2]])
+    at_time(109, take_stats)
 
     for _, _, calls in sorted(events, key=lambda e: e[:2]):
         for call in calls:
@@ -359,7 +388,7 @@
             copy.wait_send()
         else:
             pl.when(when)(copy.wait_send)
-    for q in range(4):
+    for q in range(STRIPS):
         pl.when(yh == 0)(edges[q].wait_send)
 
 
@@ -395,14 +424,14 @@
             dma((4,)), dma((4,)),
             dma((3, 8)), dma((3, 8)),
             dma((8, 4)), dma((8, 4)),
-            dma((2, 4, 4)), dma((2, 4, 4)),
-            dma((4,)), dma((4,)),
-            dma((4,)), dma((4,)),
-            dma((4,)), dma((4,)),
+            dma((2, STRIPS, 4)), dma((2, STRIPS, 4)),
+            dma((STRIPS,)), dma((STRIPS,)),
+            dma((STRIPS,)), dma((STRIPS,)),
+            dma((STRIPS,)), dma((STRIPS,)),
             dma((3,)), dma((3,)),
         ],
         compiler_params=pltpu.CompilerParams(
-            collective_id=0, has_side_effects=True, vmem_limit_bytes=48 * 2**20
+            collective_id=0, has_side_effects=True, vmem_limit_bytes=60 * 2**20
         ),
         cost_estimate=pl.CostEstimate(
             flops=2 * rows * 2 * rows * ZS * days, bytes_accessed=4 * rows * rows, transcendentals=0

time: 131 us -> 140 us (1.069)
  the two profiles are of different devices: /device:TPU:104 before, /device:TPU:4 now
where the time goes in v2:
time: 140 us
  Pallas kernels  135 us (96%)
  other arithmetic  3.92 us (3%)
    pallas_call x1, Pallas kernels, local(): pl.pallas_call(kernel, out_shape=(jax.ShapeDtypeStruct((rows, rows), f32)...  135 us
    div x1, other arithmetic, local(): return covar / jnp.sqrt(rain_var[:, None] * flow_var[None, :])  3 us

profile of v2, /device:TPU:4, one launch (start us, length us, event | category | flops | bytes accessed | tf_op | source)
XLA Modules:
  0.0 139.6 jit_solution(15061363445419031464)
XLA Ops:
  0.7 135.0 %shard_map.37 = (f32[640,640]{1,0:T(8,128)}, f32[8,640]{1,0:T(8,128)}) custom-call(s32[1]{0:T(128)S(6)} %copy.4.lag_ref, bf16[640,512]{1,0:T(8,128)(2,1)} %rain_ref.1, bf16[640,512]{1,0:T(8,128)(2,1)} %flow_ref.1), custom_call_target="tpu_custom_call" | custom-call | flops 6710886400 | bytes 1638400 | tf_op jit(solution)/shard_map/pallas_call | solution.py:399
  135.7 0.9 slice_reduce_fusion.2
  136.6 3.0 %rsqrt_multiply_fusion = f32[640,640]{1,0:T(8,128)} fusion(f32[640,640]{1,0:T(8,128)} %get-tuple-element.7, f32[640]{0:T(1024)S(1)} %get-tuple-element.10, f32[640]{0:T(1024)S(1)} %divide_subtract_fusion, f32[]{:T(128)} %bitcast, f32[640]{0:T(1024)S(1)} %get-tuple-element.9, f32[640]{0:T(1024)S(1)} %get-tuple-element.12), kind=kLoop, calls=%fused_computation | loop fusion | flops 2048000 | bytes 3287044 | tf_op jit(solution)/shard_map/div | solution.py:446
  (1 shorter events, 0.0 us)

commit v3 on v1

v3 whole, which is shorter than its diff:
```python
import jax
import jax.numpy as jnp
from jax import lax
from jax.experimental import pallas as pl
from jax.experimental.pallas import tpu as pltpu
from jax.sharding import PartitionSpec as P

XS, ZS, LANES = 4, 8, 128
ORDER = (0, 1, 3, 2)
BOUNDS = (0, 192, 384, 512, 640)
STRIPS = len(BOUNDS) - 1
(
    SPREAD, ROLL, RING_START, SWAP, RING, ARRIVE_OWN, ARRIVE_NEAR, ARRIVE_X, LATE, MULTIPLY, GIVE, HAND_ON, FSTAT, SHARE, FINISH, TAKE,
) = range(16)
SCHEDULE = (
    (SPREAD,), (ROLL,), (RING_START, 0), (RING_START, 1), (SWAP, 3), (SWAP, 1), (SWAP, 0), (RING, 0, 0, 1),
    (ARRIVE_OWN, 0), (RING, 1, 0, 1), (ARRIVE_OWN, 1), (RING, 1, 0, 2), (ARRIVE_NEAR, 0), (SWAP, 2), (ARRIVE_OWN, 2),
    (ARRIVE_X, 0, 1), (ARRIVE_NEAR, 2), (RING_START, 2), (ARRIVE_X, 0, 2), (RING, 1, 1, 1), (LATE, 0),
    (RING, 0, 0, 2), (ARRIVE_NEAR, 1), (ARRIVE_X, 2, 1), (ARRIVE_OWN, 3), (ARRIVE_X, 0, 3), (ARRIVE_X, 1, 2),
    (RING, 1, 0, 3), (RING, 1, 1, 2), (RING, 0, 2, 1), (ARRIVE_X, 1, 1), (ARRIVE_X, 2, 2), (RING, 0, 1, 1),
    (RING, 0, 0, 3), (RING, 1, 2, 1), (ARRIVE_X, 2, 3), (RING, 1, 1, 3), (ARRIVE_NEAR, 3), (RING, 1, 2, 2),
    (ARRIVE_X, 3, 2), (ARRIVE_X, 1, 3), (LATE, 2), (ARRIVE_X, 3, 3), (RING, 0, 1, 2), (ARRIVE_X, 3, 1),
    (RING_START, 3), (ARRIVE_X, 4, 2), (RING, 1, 1, 4), (LATE, 1), (ARRIVE_X, 4, 1), (RING, 0, 2, 2), (RING, 1, 3, 1),
    (ARRIVE_X, 6, 2), (LATE, 3), (RING, 1, 2, 3), (RING, 0, 1, 3), (RING, 0, 0, 4), (MULTIPLY, 0, 0, 1, 1),
    (MULTIPLY, 0, 0, 4, 4), (ARRIVE_X, 4, 3), (RING, 0, 3, 1), (MULTIPLY, 0, 0, 2, 3), (GIVE, 0), (GIVE, 1),
    (RING, 1, 3, 2), (ARRIVE_X, 5, 2), (ARRIVE_X, 6, 1), (MULTIPLY, 1, 0, 1, 1), (ARRIVE_X, 7, 2), (ARRIVE_X, 5, 1),
    (RING, 0, 3, 2), (ARRIVE_X, 5, 3), (ARRIVE_X, 6, 3), (ARRIVE_X, 7, 1), (RING, 0, 2, 3), (RING, 1, 3, 3),
    (RING, 0, 2, 4), (RING, 0, 3, 3), (ARRIVE_X, 7, 3), (HAND_ON, 0), (HAND_ON, 1), (MULTIPLY, 1, 0, 3, 3),
    (RING, 1, 3, 4), (MULTIPLY, 1, 0, 2, 2), (MULTIPLY, 1, 0, 4, 4), (GIVE, 2), (GIVE, 3), (FSTAT, 0),
    (MULTIPLY, 0, 1, 1, 4), (HAND_ON, 2), (HAND_ON, 3), (FSTAT, 1), (SHARE,), (MULTIPLY, 1, 1, 1, 4), (FINISH, 0),
    (FINISH, 1), (TAKE,), (FINISH, 2), (FINISH, 3),
)


def kernel(
    lag_ref, rain_v, flow_v, cross_ref, stat_ref,
    stage, rain_all, flow_all, acc, relay, final,
    rain_part, flow_part, stat_send, stat_recv,
    s1, r1, s2, r2, s3, r3, sx, rx, sc, rc, sr, rr, se, re, sg, rg, sf, rf, st, rt,
):
    rows, days = rain_v.shape
    piece = rows // XS
    assert rows == BOUNDS[-1]
    tiles = days // LANES
    lag = lag_ref[0]
    blk, tm = lax.axis_index("blk"), lax.axis_index("tm")
    yl, x, c = lax.div(blk, 8), lax.rem(lax.div(blk, 2), 4), lax.rem(blk, 2)
    yh, z = lax.div(tm, 8), lax.rem(tm, 8)
    zp, zo = lax.div(z, 2), lax.rem(z, 2)
    other = 1 - yh

    def dev(yl_=None, x_=None, c_=None, yh_=None, z_=None):
        b = (yl if yl_ is None else yl_) * 8 + (x if x_ is None else x_) * 2 + (c if c_ is None else c_)
        t = (yh if yh_ is None else yh_) * 8 + (z if z_ is None else z_)
        return (b, t)

    def xo(d):
        return lax.rem(x + d, XS)

    def zo_(d):
        return lax.rem(z + d + ZS, ZS)

    y = 2 * yh + yl
    yu, yd = lax.rem(y + 1, 4), lax.rem(y + 3, 4)
    up = dev(yl_=lax.rem(yu, 2), yh_=lax.div(yu, 2))
    down = dev(yl_=lax.rem(yd, 2), yh_=lax.div(yd, 2))
    near = dev(yl_=1 - yl)
    sibling = dev(c_=1 - c)
    far = dev(yh_=other)
    far_sibling = dev(yh_=other, c_=1 - c)
    right, left = dev(x_=xo(1)), dev(x_=xo(3))
    ahead, behind = dev(z_=zo_(1)), dev(z_=zo_(-1))

    def swap_pair(k):
        return lax.rem(zp + k, 4)

    def swap_dev(k):
        return dev(z_=2 * swap_pair(k) + c, c_=zo)

    def rcopy(src, dst, send, recv, to):
        return pltpu.make_async_remote_copy(
            src_ref=src, dst_ref=dst, send_sem=send, recv_sem=recv,
            device_id=to, device_id_type=pl.DeviceIdType.MESH,
        )

    pending = []

    def send(copy, when=None):
        if when is None:
            copy.start()
        else:
            pl.when(when)(copy.start)
        pending.append((copy, when))

    crossed = c != zo
    barrier = pltpu.get_barrier_semaphore()
    partners = [dev(x_=xo(d)) for d in (1, 2, 3)]
    partners += [ahead, behind, up, down, far, far_sibling, sibling]
    partners += [swap_dev(k) for k in (1, 2, 3)]

    def greet(to):
        pl.semaphore_signal(barrier, inc=1, device_id=to, device_id_type=pl.DeviceIdType.MESH)

    for to in partners:
        greet(to)

    @pl.when(crossed)
    def _():
        greet(swap_dev(0))

    pl.semaphore_wait(barrier, len(partners) + jnp.where(crossed, 1, 0))

    def part(ref, i):
        return ref.at[pl.ds(pl.multiple_of(i * piece, piece), piece), :]

    def cell(zd, half, col):
        return flow_all.at[lax.rem(zd, 2), lax.div(zd, 2), half, pl.ds(pl.multiple_of(col * piece, piece), piece), :]

    def spread():
        pltpu.make_async_copy(part(flow_v, x), stage.at[0], r1.at[0]).start()
        for d in (1, 3, 2):
            send(rcopy(part(flow_v, xo(d)), stage.at[d], s1.at[d], r1.at[d], dev(x_=xo(d))))

    def roll():
        i0 = lax.broadcasted_iota(jnp.int32, (2 * LANES, LANES), 0)
        i1 = lax.broadcasted_iota(jnp.int32, (2 * LANES, LANES), 1)
        shift = jnp.where(i0 == i1 + LANES - lag, 1.0, 0.0).astype(jnp.bfloat16)
        for j in range(tiles):
            p = (j + tiles - 1) % tiles
            two = jnp.concatenate(
                [rain_v[:, p * LANES:(p + 1) * LANES], rain_v[:, j * LANES:(j + 1) * LANES]], axis=1
            )
            rain_all[z + 1, :, j * LANES:(j + 1) * LANES] = jnp.dot(
                two, shift, preferred_element_type=jnp.float32
            ).astype(jnp.bfloat16)

    def strip_of(chunk, q):
        return rain_all.at[chunk + 1, BOUNDS[q]:BOUNDS[q + 1], :]

    edges = [
        rcopy(
            rain_all.at[ZS, BOUNDS[q]:BOUNDS[q + 1], 0:LANES],
            rain_all.at[0, BOUNDS[q]:BOUNDS[q + 1], 0:LANES],
            se.at[q], re.at[q], far,
        )
        for q in range(STRIPS)
    ]

    @pl.when(yh == 0)
    def _():
        rain_all[0, :, 0:LANES] = jnp.zeros((rows, LANES), jnp.bfloat16)

    def pass_edge(chunk, q):
        pl.when((chunk == ZS - 1) & (yh == 0))(edges[q].start)

    def ring_copy(way, q, s):
        chunk = zo_(1 - s) if way == 0 else zo_(s - 1)
        at = strip_of(chunk, q)
        return rcopy(at, at, sr.at[way, q, s - 1], rr.at[way, q, s - 1], ahead if way == 0 else behind)

    def reach(way, q):
        return 4 if (q + way) % 2 == 0 else 3

    def ring_start(q):
        pass_edge(z, q)
        for way in (0, 1):
            send(ring_copy(way, q, 1))

    def ring_arrive(way, q, s):
        chunk = zo_(-s) if way == 0 else zo_(s)
        at = strip_of(chunk, q)
        rcopy(at, at, sr.at[way, q, s - 1], rr.at[way, q, s - 1], behind).wait_recv()
        if s < reach(way, q):
            send(ring_copy(way, q, s + 1))
        pass_edge(chunk, q)

    def swap(k):
        d = lax.rem(x - swap_pair(k) + XS, XS)
        src = stage.at[d]
        rcopy(src, src, s1.at[0], r1.at[d], right).wait_recv()
        dst = cell(z, yl, x)
        remote = rcopy(src, dst, s2.at[k], r2.at[k], swap_dev(k))
        if k == 0:
            send(remote, crossed)
            pl.when(jnp.logical_not(crossed))(pltpu.make_async_copy(src, dst, r2.at[0]).start)
        else:
            send(remote)

    def home(k):
        return 2 * lax.rem(zp - k + 4, 4) + c

    first = yl == other

    got = {}

    def sibling_copy(half, o):
        col = xo((0, 3, 1, 2)[o])
        at = flow_all.at[c, :, half, pl.ds(pl.multiple_of(col * piece, piece), piece), :]
        return rcopy(at, at, sc.at[half, o], rc.at[half, o], sibling)

    def to_sibling(group, half, o):
        got[group, o] = got.get((group, o), 0) + 1
        if got[group, o] == 4:
            send(sibling_copy(half, o))

    def along_x(at, j, when=None):
        send(rcopy(at, at, sx.at[0, j], rx.at[0, j], right), when)
        send(rcopy(at, at, sx.at[1, j], rx.at[1, j], left), when)

    def half_of(j):
        return other if j < 4 else yh

    def arrive_own(i):
        k = ORDER[i]
        at = cell(home(k), yl, x)
        rcopy(at, at, s2.at[k], r2.at[k], right).wait_recv()
        send(rcopy(at, at, s3.at[k], r3.at[k], near))
        along_x(at, i, first)
        to_sibling(ARRIVE_OWN, yl, 0)

    def arrive_near(i):
        k = ORDER[i]
        at = cell(home(k), 1 - yl, x)
        rcopy(at, at, s3.at[k], r3.at[k], near).wait_recv()
        along_x(at, i, jnp.logical_not(first))
        to_sibling(ARRIVE_NEAR, 1 - yl, 0)

    def late(i):
        along_x(cell(home(ORDER[i]), yh, x), i + 4)

    def arrive_x(j, o):
        at = cell(home(ORDER[j % 4]), half_of(j), xo({1: 3, 2: 1, 3: 2}[o]))
        rcopy(at, at, sx.at[o - 1, j], rx.at[o - 1, j], right).wait_recv()
        if o == 1 and j % 2 == 0:
            send(rcopy(at, at, sx.at[2, j], rx.at[2, j], right))
        if o == 2 and j % 2 == 1:
            send(rcopy(at, at, sx.at[2, j], rx.at[2, j], left))
        to_sibling(j // 4, half_of(j), o)

    def flow_ready(h):
        half = other if h == 0 else yh
        for o in range(4):
            sibling_copy(half, o).wait_recv()

    def folded(v):
        return sum(v[:, t * LANES:(t + 1) * LANES] for t in range(tiles))

    def multiply(lo, hi, h, low, high, start):
        at = slice(lo, hi)
        half = other if h == 0 else yh
        lane = lax.broadcasted_iota(jnp.int32, (hi - lo, LANES), 1)
        if start:
            for t in range(lo // LANES, hi // LANES):
                acc[h, t] = jnp.zeros((rows, LANES), jnp.float32)

        def step(s, carry):
            used, cells = [], []
            for zd in (zo_(s), zo_(1 - s)):
                before = rain_all[zd, at, 0:LANES].astype(jnp.float32)
                here = rain_all[zd + 1, at, 0:LANES].astype(jnp.float32)
                head = jnp.where(lane < lag, before, here).astype(jnp.bfloat16)
                used.append(jnp.concatenate([head, rain_all[zd + 1, at, LANES:]], axis=1))
                cells.append(flow_all[lax.rem(zd, 2), lax.div(zd, 2), half])
            product = lax.dot_general(
                jnp.concatenate(cells, axis=1), jnp.concatenate(used, axis=1),
                (((1,), (1,)), ((), ())), preferred_element_type=jnp.float32,
            )
            for t in range(lo // LANES, hi // LANES):
                acc[h, t] += product[:, t * LANES - lo:(t + 1) * LANES - lo]
            if h == 0:
                wide = [u.astype(jnp.float32) for u in used]
                rain_part[0, at, :] += sum(folded(u) for u in wide)
                rain_part[1, at, :] += sum(folded(u * u) for u in wide)
            return carry

        lax.fori_loop(low, high + 1, step, 0)

    def flow_stats(h):
        half = other if h == 0 else yh
        blocks = rows // LANES
        lanes = lax.broadcasted_iota(jnp.int32, (LANES, LANES), 1)

        def step(i, carry):
            m = lax.div(i, blocks)
            zd = 2 * m + c
            at = pl.ds(pl.multiple_of(lax.rem(i, blocks) * LANES, LANES), LANES)
            wide = flow_all[c, m, half, at, :].astype(jnp.float32)
            skip = jnp.where((yh == 0) & (zd == 0), lag, 0)
            head = jnp.where(lanes < skip, 0.0, wide[:, 0:LANES])
            wide = jnp.concatenate([head, wide[:, LANES:]], axis=1)
            flow_part[h, 0, at, :] += folded(wide)
            flow_part[h, 1, at, :] += folded(wide * wide)
            return carry

        lax.fori_loop(0, 4 * blocks, step, 0)

    def rows_of(ref, b):
        return jnp.sum(ref[b * LANES:(b + 1) * LANES, :].T, axis=0, keepdims=True)

    def share_stats():
        for b in range(rows // LANES):
            rs, rq = rows_of(rain_part.at[0], b), rows_of(rain_part.at[1], b)
            zero = jnp.zeros((4, LANES), jnp.float32)
            for i, h in ((0, 1), (1, 0)):
                fs, fq = rows_of(flow_part.at[h, 0], b), rows_of(flow_part.at[h, 1], b)
                stat_send[i, :, b * LANES:(b + 1) * LANES] = jnp.concatenate([fs, fq, rs, rq, zero], axis=0)
        for i, (src, to) in enumerate(((0, sibling), (1, far), (1, far_sibling))):
            send(rcopy(stat_send.at[src], stat_recv.at[i], st.at[i], rt.at[i], to))

    def take_stats():
        for i in range(3):
            at = stat_recv.at[i]
            rcopy(at, at, st.at[i], rt.at[i], sibling).wait_recv()
        is_flow = lax.broadcasted_iota(jnp.int32, (8, rows), 0) < 2
        halves = stat_recv[0] + stat_recv[2]
        stat_ref[...] = stat_send[0] + stat_recv[1] + jnp.where(is_flow, halves, 0.0)

    parcels = (((0, 0, rows), (2, 0, 384)), ((1, 0, rows), (2, 384, rows)), ((3, 0, rows),), ((4, 0, rows),))

    def way_of(q):
        return up if q % 2 == 0 else down

    def give(q):
        for n, (t, lo, hi) in enumerate(parcels[q]):
            src, dst = acc.at[0, t, lo:hi, :], relay.at[t, lo:hi, :]
            send(rcopy(src, dst, sg.at[q, n], rg.at[q, n], way_of(q)))

    def hand_on(q):
        for n, (t, lo, hi) in enumerate(parcels[q]):
            at = relay.at[t, lo:hi, :]
            rcopy(at, at, sg.at[q, n], rg.at[q, n], up).wait_recv()
            send(rcopy(at, final.at[t, lo:hi, :], sf.at[q, n], rf.at[q, n], way_of(q)))

    def finish(q):
        for n, (t, lo, hi) in enumerate(parcels[q]):
            ref = final.at[t, lo:hi, :]
            rcopy(ref, ref, sf.at[q, n], rf.at[q, n], up).wait_recv()
            for i in range(lo, hi, LANES):
                block = acc[1, t, i:i + LANES, :] + final[t, i:i + LANES, :]
                cross_ref[t * LANES:(t + 1) * LANES, i:i + LANES] = block.T

    def edge_ready(wave, s):
        for zd in (zo_(s), zo_(1 - s)):

            @pl.when((zd == 0) & (yh == 1))
            def _():
                for q in wave:
                    edges[q].wait_recv()

    seen = set()

    def once(*key):
        new = key not in seen
        seen.add(key)
        return new

    def step(kind, *at):
        if kind in (MULTIPLY, FSTAT):
            h = at[1] if kind == MULTIPLY else at[0]
            if once(FSTAT, h):
                flow_ready(h)
        if kind == MULTIPLY:
            w, h, low, high = at
            for s in range(low, high + 1):
                if once(RING, w, s):
                    edge_ready((2 * w, 2 * w + 1), s)
            multiply(BOUNDS[2 * w], BOUNDS[2 * w + 2], h, low, high, once(MULTIPLY, w, h))
        else:
            steps[kind](*at)

    steps = {
        SPREAD: spread, ROLL: roll, SWAP: swap, RING_START: ring_start, RING: ring_arrive,
        ARRIVE_OWN: arrive_own, ARRIVE_NEAR: arrive_near, LATE: late, ARRIVE_X: arrive_x, FSTAT: flow_stats,
        GIVE: give, HAND_ON: hand_on, SHARE: share_stats, FINISH: finish, TAKE: take_stats,
    }
    def drain():
        for copy, when in pending:
            if when is None:
                copy.wait_send()
            else:
                pl.when(when)(copy.wait_send)
        pending.clear()

    def drain_edges():
        for q in range(STRIPS):
            pl.when(yh == 0)(edges[q].wait_send)

    rain_part[...] = jnp.zeros(rain_part.shape, jnp.float32)
    flow_part[...] = jnp.zeros(flow_part.shape, jnp.float32)
    for item in SCHEDULE:
        if item[0] in (TAKE, FINISH) and once(FINISH):
            drain_edges()
            drain()
        step(*item)

    drain()


def local(rainfall, runoff, lag_days):
    rows, days = rainfall.shape
    dma = pltpu.SemaphoreType.DMA
    bf16, f32 = jnp.bfloat16, jnp.float32
    cross, stats = pl.pallas_call(
        kernel,
        out_shape=(jax.ShapeDtypeStruct((rows, rows), f32), jax.ShapeDtypeStruct((8, rows), f32)),
        in_specs=[
            pl.BlockSpec(memory_space=pltpu.SMEM),
            pl.BlockSpec(memory_space=pltpu.VMEM),
            pl.BlockSpec(memory_space=pltpu.VMEM),
        ],
        out_specs=[pl.BlockSpec(memory_space=pltpu.VMEM)] * 2,
        scratch_shapes=[
            pltpu.VMEM((XS, rows // XS, days), bf16),
            pltpu.VMEM((ZS + 1, rows, days), bf16),
            pltpu.VMEM((2, ZS // 2, 2, rows, days), bf16),
            pltpu.VMEM((2, rows // LANES, rows, LANES), f32),
            pltpu.VMEM((rows // LANES, rows, LANES), f32),
            pltpu.VMEM((rows // LANES, rows, LANES), f32),
            pltpu.VMEM((2, rows, LANES), f32),
            pltpu.VMEM((2, 2, rows, LANES), f32),
            pltpu.VMEM((2, 8, rows), f32),
            pltpu.VMEM((3, 8, rows), f32),
            dma((4,)), dma((4,)),
            dma((4,)), dma((4,)),
            dma((4,)), dma((4,)),
            dma((3, 8)), dma((3, 8)),
            dma((2, 4)), dma((2, 4)),
            dma((2, STRIPS, 4)), dma((2, STRIPS, 4)),
            dma((STRIPS,)), dma((STRIPS,)),
            dma((4, 2)), dma((4, 2)),
            dma((4, 2)), dma((4, 2)),
            dma((3,)), dma((3,)),
        ],
        compiler_params=pltpu.CompilerParams(
            collective_id=0, has_side_effects=True, vmem_limit_bytes=48 * 2**20
        ),
        cost_estimate=pl.CostEstimate(
            flops=2 * rows * 2 * rows * ZS * days, bytes_accessed=4 * rows * rows, transcendentals=0
        ),
    )(lag_days, rainfall, runoff)
    total = days * lax.axis_size("tm")
    samples = (total - lag_days[0]).astype(f32)
    flow_sum, flow_square, rain_sum, rain_square = stats[0], stats[1], stats[2], stats[3]
    covar = cross - rain_sum[:, None] * flow_sum[None, :] / samples
    rain_var = rain_square - rain_sum * rain_sum / samples
    flow_var = flow_square - flow_sum * flow_sum / samples
    return covar / jnp.sqrt(rain_var[:, None] * flow_var[None, :])


def solution(mesh):
    placed = (P("blk", "tm"), P("blk", "tm"), P())
    return jax.shard_map(
        local, mesh=mesh, in_specs=placed, out_specs=P("blk", "tm"), check_vma=False
    )
```

time: 131 us -> 129 us (0.985)
  Pallas kernels: 126 us -> 123 us
    pallas_call x1, Pallas kernels: 126 us -> 123 us  [local(): pl.pallas_call(kernel, out_shape=(jax.ShapeDtypeStruct((rows, rows), f32)...]
where the time goes in v3:
time: 129 us; the launch traced here: 128 us
  Pallas kernels  123 us (95%)
  local copies, waits for them, and re-layouts  2.17 us (2%)
  other arithmetic  1.61 us (1%)
    pallas_call x1, Pallas kernels, local(): pl.pallas_call(kernel, out_shape=(jax.ShapeDtypeStruct((rows, rows), f32)...  123 us

profile of v3, /device:TPU:104, one launch (start us, length us, event | category | flops | bytes accessed | tf_op | source)
XLA Modules:
  0.0 127.7 jit_solution(5078919031077112760)
XLA Ops:
  0.7 0.0 copy-start
  0.7 1.1 copy-done
  1.7 0.0 copy-start.1
  1.7 1.1 copy-done.1
  2.8 123.2 %shard_map.37 = (f32[640,640]{1,0:T(8,128)S(1)}, f32[8,640]{1,0:T(8,128)S(1)}) custom-call(s32[1]{0:T(128)S(6)} %copy.4.lag_ref, bf16[640,512]{1,0:T(8,128)(2,1)S(1)} %copy-done, bf16[640,512]{1,0:T(8,128)(2,1)S(1)} %copy-done.1), custom_call_target="tpu_custom_call" | custom-call | flops 6710886400 | bytes 1638400 | tf_op jit(solution)/shard_map/pallas_call | solution.py:403
  126.1 1.6 %rsqrt_multiply_fusion = f32[640,640]{1,0:T(8,128)} fusion(f32[640,640]{1,0:T(8,128)S(1)} %get-tuple-element.7, f32[640]{0:T(1024)S(1)} %get-tuple-element.10, f32[640]{0:T(1024)S(1)} %divide_subtract_fusion, f32[]{:T(128)} %bitcast, f32[640]{0:T(1024)S(1)} %get-tuple-element.9, f32[640]{0:T(1024)S(1)} %get-tuple-element.12), kind=kLoop, calls=%fused_computation | loop fusion | flops 2048000 | bytes 3287044 | tf_op jit(solution)/shard_map/div | solution.py:447
  (2 shorter events, 0.0 us)
Async XLA Ops:
  0.7 1.1 copy-start
  1.7 1.1 copy-start.1

commit v4 on v3

--- a/solution.py
+++ b/solution.py
@@ -7,28 +7,29 @@
 
 XS, ZS, LANES = 4, 8, 128
 ORDER = (0, 1, 3, 2)
-BOUNDS = (0, 192, 384, 512, 640)
+BOUNDS = (0, 176, 352, 496, 640)
 STRIPS = len(BOUNDS) - 1
+CUT = 32
 (
-    SPREAD, ROLL, RING_START, SWAP, RING, ARRIVE_OWN, ARRIVE_NEAR, ARRIVE_X, LATE, MULTIPLY, GIVE, HAND_ON, FSTAT, SHARE, FINISH, TAKE,
-) = range(16)
+    SPREAD, ROLL, RING_START, SWAP, RING, ARRIVE_OWN, ARRIVE_NEAR, ARRIVE_X, LATE, MULTIPLY, GIVE, RSTAT, FSTAT, HAND_ON, SHARE, FINISH, TAKE,
+) = range(17)
 SCHEDULE = (
-    (SPREAD,), (ROLL,), (RING_START, 0), (RING_START, 1), (SWAP, 3), (SWAP, 1), (SWAP, 0), (RING, 0, 0, 1),
-    (ARRIVE_OWN, 0), (RING, 1, 0, 1), (ARRIVE_OWN, 1), (RING, 1, 0, 2), (ARRIVE_NEAR, 0), (SWAP, 2), (ARRIVE_OWN, 2),
-    (ARRIVE_X, 0, 1), (ARRIVE_NEAR, 2), (RING_START, 2), (ARRIVE_X, 0, 2), (RING, 1, 1, 1), (LATE, 0),
-    (RING, 0, 0, 2), (ARRIVE_NEAR, 1), (ARRIVE_X, 2, 1), (ARRIVE_OWN, 3), (ARRIVE_X, 0, 3), (ARRIVE_X, 1, 2),
-    (RING, 1, 0, 3), (RING, 1, 1, 2), (RING, 0, 2, 1), (ARRIVE_X, 1, 1), (ARRIVE_X, 2, 2), (RING, 0, 1, 1),
-    (RING, 0, 0, 3), (RING, 1, 2, 1), (ARRIVE_X, 2, 3), (RING, 1, 1, 3), (ARRIVE_NEAR, 3), (RING, 1, 2, 2),
-    (ARRIVE_X, 3, 2), (ARRIVE_X, 1, 3), (LATE, 2), (ARRIVE_X, 3, 3), (RING, 0, 1, 2), (ARRIVE_X, 3, 1),
-    (RING_START, 3), (ARRIVE_X, 4, 2), (RING, 1, 1, 4), (LATE, 1), (ARRIVE_X, 4, 1), (RING, 0, 2, 2), (RING, 1, 3, 1),
-    (ARRIVE_X, 6, 2), (LATE, 3), (RING, 1, 2, 3), (RING, 0, 1, 3), (RING, 0, 0, 4), (MULTIPLY, 0, 0, 1, 1),
-    (MULTIPLY, 0, 0, 4, 4), (ARRIVE_X, 4, 3), (RING, 0, 3, 1), (MULTIPLY, 0, 0, 2, 3), (GIVE, 0), (GIVE, 1),
-    (RING, 1, 3, 2), (ARRIVE_X, 5, 2), (ARRIVE_X, 6, 1), (MULTIPLY, 1, 0, 1, 1), (ARRIVE_X, 7, 2), (ARRIVE_X, 5, 1),
-    (RING, 0, 3, 2), (ARRIVE_X, 5, 3), (ARRIVE_X, 6, 3), (ARRIVE_X, 7, 1), (RING, 0, 2, 3), (RING, 1, 3, 3),
-    (RING, 0, 2, 4), (RING, 0, 3, 3), (ARRIVE_X, 7, 3), (HAND_ON, 0), (HAND_ON, 1), (MULTIPLY, 1, 0, 3, 3),
-    (RING, 1, 3, 4), (MULTIPLY, 1, 0, 2, 2), (MULTIPLY, 1, 0, 4, 4), (GIVE, 2), (GIVE, 3), (FSTAT, 0),
-    (MULTIPLY, 0, 1, 1, 4), (HAND_ON, 2), (HAND_ON, 3), (FSTAT, 1), (SHARE,), (MULTIPLY, 1, 1, 1, 4), (FINISH, 0),
-    (FINISH, 1), (TAKE,), (FINISH, 2), (FINISH, 3),
+    (SPREAD,), (ROLL,), (RING_START, 0), (RING_START, 1), (SWAP, 1), (SWAP, 0), (SWAP, 3), (RING, 1, 0, 1), (SWAP, 2),
+    (ARRIVE_OWN, 0), (ARRIVE_OWN, 1), (ARRIVE_OWN, 2), (RING, 1, 0, 2), (ARRIVE_NEAR, 0), (ARRIVE_NEAR, 1),
+    (RING_START, 2), (ARRIVE_X, 0, 2), (ARRIVE_NEAR, 2), (ARRIVE_X, 0, 1), (RING, 1, 1, 1), (RING, 0, 0, 1),
+    (RING, 0, 0, 2), (LATE, 0), (ARRIVE_X, 2, 1), (RING, 0, 2, 1), (ARRIVE_OWN, 3), (RING, 1, 1, 2), (ARRIVE_X, 1, 2),
+    (RING, 1, 0, 3), (ARRIVE_X, 0, 3), (RING, 1, 2, 1), (ARRIVE_X, 2, 2), (RING, 0, 1, 1), (ARRIVE_NEAR, 3),
+    (RING, 0, 0, 3), (RING, 1, 2, 2), (RING, 1, 1, 3), (ARRIVE_X, 3, 2), (ARRIVE_X, 3, 1), (ARRIVE_X, 2, 3),
+    (ARRIVE_X, 1, 1), (LATE, 1), (RING, 1, 2, 3), (ARRIVE_X, 1, 3), (LATE, 2), (RING, 0, 1, 2), (RING_START, 3),
+    (RING, 0, 0, 4), (ARRIVE_X, 3, 3), (ARRIVE_X, 4, 1), (RING, 0, 1, 3), (RING, 0, 2, 2), (RING, 1, 1, 4),
+    (RING, 1, 3, 1), (ARRIVE_X, 4, 2), (LATE, 3), (MULTIPLY, 0, 0, 4, 4), (MULTIPLY, 0, 0, 1, 1), (RING, 0, 3, 1),
+    (MULTIPLY, 0, 0, 2, 3), (RING, 1, 3, 2), (ARRIVE_X, 6, 2), (GIVE, 1), (GIVE, 0), (MULTIPLY, 1, 0, 1, 1),
+    (RSTAT, 0), (ARRIVE_X, 4, 3), (ARRIVE_X, 5, 2), (ARRIVE_X, 6, 1), (RING, 0, 3, 2), (ARRIVE_X, 7, 2), (FSTAT, 0),
+    (RING, 0, 2, 3), (RING, 1, 3, 3), (HAND_ON, 0), (ARRIVE_X, 6, 3), (HAND_ON, 1), (ARRIVE_X, 5, 1), (RING, 0, 3, 3),
+    (ARRIVE_X, 7, 1), (RING, 1, 3, 4), (MULTIPLY, 1, 0, 3, 3), (ARRIVE_X, 7, 3), (ARRIVE_X, 5, 3), (RING, 0, 2, 4),
+    (MULTIPLY, 1, 0, 2, 2), (MULTIPLY, 1, 0, 4, 4), (GIVE, 2), (GIVE, 3), (RSTAT, 1), (FSTAT, 1),
+    (MULTIPLY, 0, 1, 1, 4), (SHARE,), (HAND_ON, 3), (HAND_ON, 2), (MULTIPLY, 1, 1, 1, 4), (FINISH, 0), (FINISH, 1),
+    (FINISH, 3), (TAKE,), (FINISH, 2),
 )
 
 
@@ -250,30 +251,38 @@
         half = other if h == 0 else yh
         lane = lax.broadcasted_iota(jnp.int32, (hi - lo, LANES), 1)
         if start:
-            for t in range(lo // LANES, hi // LANES):
-                acc[h, t] = jnp.zeros((rows, LANES), jnp.float32)
-
-        def step(s, carry):
-            used, cells = [], []
-            for zd in (zo_(s), zo_(1 - s)):
-                before = rain_all[zd, at, 0:LANES].astype(jnp.float32)
-                here = rain_all[zd + 1, at, 0:LANES].astype(jnp.float32)
-                head = jnp.where(lane < lag, before, here).astype(jnp.bfloat16)
-                used.append(jnp.concatenate([head, rain_all[zd + 1, at, LANES:]], axis=1))
-                cells.append(flow_all[lax.rem(zd, 2), lax.div(zd, 2), half])
-            product = lax.dot_general(
-                jnp.concatenate(cells, axis=1), jnp.concatenate(used, axis=1),
-                (((1,), (1,)), ((), ())), preferred_element_type=jnp.float32,
+            acc[h, at, :] = jnp.zeros((hi - lo, rows), jnp.float32)
+
+        def step(i, carry):
+            s = low + lax.div(i, 2)
+            zd = zo_(jnp.where(lax.rem(i, 2) == 0, s, 1 - s))
+            before = rain_all[zd, at, 0:LANES].astype(jnp.float32)
+            here = rain_all[zd + 1, at, 0:LANES].astype(jnp.float32)
+            head = jnp.where(lane < lag, before, here).astype(jnp.bfloat16)
+            used = jnp.concatenate([head, rain_all[zd + 1, at, LANES:]], axis=1)
+            acc[h, at, :] += lax.dot_general(
+                used, flow_all[lax.rem(zd, 2), lax.div(zd, 2), half], (((1,), (1,)), ((), ())), preferred_element_type=jnp.float32
             )
-            for t in range(lo // LANES, hi // LANES):
-                acc[h, t] += product[:, t * LANES - lo:(t + 1) * LANES - lo]
-            if h == 0:
-                wide = [u.astype(jnp.float32) for u in used]
-                rain_part[0, at, :] += sum(folded(u) for u in wide)
-                rain_part[1, at, :] += sum(folded(u * u) for u in wide)
             return carry
 
-        lax.fori_loop(low, high + 1, step, 0)
+        lax.fori_loop(0, 2 * (high - low + 1), step, 0)
+
+    def rain_stats(w):
+        lo, hi = BOUNDS[2 * w], BOUNDS[2 * w + 2]
+        lane = lax.broadcasted_iota(jnp.int32, (CUT, LANES), 1)
+
+        def step(i, carry):
+            zd = lax.rem(i, ZS)
+            at = pl.ds(pl.multiple_of(lo + lax.div(i, ZS) * CUT, CUT), CUT)
+            before = rain_all[zd, at, 0:LANES].astype(jnp.float32)
+            wide = rain_all[zd + 1, at, :].astype(jnp.float32)
+            head = jnp.where(lane < lag, before, wide[:, 0:LANES])
+            wide = jnp.concatenate([head, wide[:, LANES:]], axis=1)
+            rain_part[0, at, :] += folded(wide)
+            rain_part[1, at, :] += folded(wide * wide)
+            return carry
+
+        lax.fori_loop(0, ZS * (hi - lo) // CUT, step, 0)
 
     def flow_stats(h):
         half = other if h == 0 else yh
@@ -315,29 +324,22 @@
         halves = stat_recv[0] + stat_recv[2]
         stat_ref[...] = stat_send[0] + stat_recv[1] + jnp.where(is_flow, halves, 0.0)
 
-    parcels = (((0, 0, rows), (2, 0, 384)), ((1, 0, rows), (2, 384, rows)), ((3, 0, rows),), ((4, 0, rows),))
-
-    def way_of(q):
-        return up if q % 2 == 0 else down
+    def strip_at(ref, q):
+        return ref.at[BOUNDS[q]:BOUNDS[q + 1], :]
 
     def give(q):
-        for n, (t, lo, hi) in enumerate(parcels[q]):
-            src, dst = acc.at[0, t, lo:hi, :], relay.at[t, lo:hi, :]
-            send(rcopy(src, dst, sg.at[q, n], rg.at[q, n], way_of(q)))
+        send(rcopy(strip_at(acc.at[0], q), strip_at(relay, q), sg.at[q], rg.at[q], up if q % 2 == 0 else down))
 
     def hand_on(q):
-        for n, (t, lo, hi) in enumerate(parcels[q]):
-            at = relay.at[t, lo:hi, :]
-            rcopy(at, at, sg.at[q, n], rg.at[q, n], up).wait_recv()
-            send(rcopy(at, final.at[t, lo:hi, :], sf.at[q, n], rf.at[q, n], way_of(q)))
+        at = strip_at(relay, q)
+        rcopy(at, at, sg.at[q], rg.at[q], up).wait_recv()
+        send(rcopy(at, strip_at(final, q), sf.at[q], rf.at[q], up if q % 2 == 0 else down))
 
     def finish(q):
-        for n, (t, lo, hi) in enumerate(parcels[q]):
-            ref = final.at[t, lo:hi, :]
-            rcopy(ref, ref, sf.at[q, n], rf.at[q, n], up).wait_recv()
-            for i in range(lo, hi, LANES):
-                block = acc[1, t, i:i + LANES, :] + final[t, i:i + LANES, :]
-                cross_ref[t * LANES:(t + 1) * LANES, i:i + LANES] = block.T
+        at = slice(BOUNDS[q], BOUNDS[q + 1])
+        ref = strip_at(final, q)
+        rcopy(ref, ref, sf.at[q], rf.at[q], up).wait_recv()
+        cross_ref[at, :] = acc[1, at, :] + final[at, :]
 
     def edge_ready(wave, s):
         for zd in (zo_(s), zo_(1 - s)):
@@ -359,18 +361,19 @@
             h = at[1] if kind == MULTIPLY else at[0]
             if once(FSTAT, h):
                 flow_ready(h)
-        if kind == MULTIPLY:
-            w, h, low, high = at
+        if kind in (MULTIPLY, RSTAT):
+            w, low, high = (at[0], at[2], at[3]) if kind == MULTIPLY else (at[0], 1, 4)
             for s in range(low, high + 1):
                 if once(RING, w, s):
                     edge_ready((2 * w, 2 * w + 1), s)
+        if kind == MULTIPLY:
             multiply(BOUNDS[2 * w], BOUNDS[2 * w + 2], h, low, high, once(MULTIPLY, w, h))
         else:
             steps[kind](*at)
 
     steps = {
         SPREAD: spread, ROLL: roll, SWAP: swap, RING_START: ring_start, RING: ring_arrive,
-        ARRIVE_OWN: arrive_own, ARRIVE_NEAR: arrive_near, LATE: late, ARRIVE_X: arrive_x, FSTAT: flow_stats,
+        ARRIVE_OWN: arrive_own, ARRIVE_NEAR: arrive_near, LATE: late, ARRIVE_X: arrive_x, FSTAT: flow_stats, RSTAT: rain_stats,
         GIVE: give, HAND_ON: hand_on, SHARE: share_stats, FINISH: finish, TAKE: take_stats,
     }
     def drain():
@@ -413,9 +416,9 @@
             pltpu.VMEM((XS, rows // XS, days), bf16),
             pltpu.VMEM((ZS + 1, rows, days), bf16),
             pltpu.VMEM((2, ZS // 2, 2, rows, days), bf16),
-            pltpu.VMEM((2, rows // LANES, rows, LANES), f32),
-            pltpu.VMEM((rows // LANES, rows, LANES), f32),
-            pltpu.VMEM((rows // LANES, rows, LANES), f32),
+            pltpu.VMEM((2, rows, rows), f32),
+            pltpu.VMEM((rows, rows), f32),
+            pltpu.VMEM((rows, rows), f32),
             pltpu.VMEM((2, rows, LANES), f32),
             pltpu.VMEM((2, 2, rows, LANES), f32),
             pltpu.VMEM((2, 8, rows), f32),
@@ -427,8 +430,8 @@
             dma((2, 4)), dma((2, 4)),
             dma((2, STRIPS, 4)), dma((2, STRIPS, 4)),
             dma((STRIPS,)), dma((STRIPS,)),
-            dma((4, 2)), dma((4, 2)),
-            dma((4, 2)), dma((4, 2)),
+            dma((STRIPS,)), dma((STRIPS,)),
+            dma((STRIPS,)), dma((STRIPS,)),
             dma((3,)), dma((3,)),
         ],
         compiler_params=pltpu.CompilerParams(

time: 129 us -> 124 us (0.961)
  the two profiles are of different devices: /device:TPU:104 before, /device:TPU:64 now
where the time goes in v4:
time: 124 us
  Pallas kernels  120 us (97%)
  local copies, waits for them, and re-layouts  2.17 us (2%)
  other arithmetic  1.61 us (1%)
    pallas_call x1, Pallas kernels, local(): pl.pallas_call(kernel, out_shape=(jax.ShapeDtypeStruct((rows, rows), f32)...  120 us

profile of v4, /device:TPU:64, one launch (start us, length us, event | category | flops | bytes accessed | tf_op | source)
XLA Modules:
  0.0 124.1 jit_solution(11028696984269819964)
XLA Ops:
  0.7 0.0 copy-start
  0.7 1.1 copy-done
  1.7 0.0 copy-start.1
  1.7 1.1 copy-done.1
  2.8 119.6 %shard_map.37 = (f32[640,640]{1,0:T(8,128)S(1)}, f32[8,640]{1,0:T(8,128)S(1)}) custom-call(s32[1]{0:T(128)S(6)} %copy.4.lag_ref, bf16[640,512]{1,0:T(8,128)(2,1)S(1)} %copy-done, bf16[640,512]{1,0:T(8,128)(2,1)S(1)} %copy-done.1), custom_call_target="tpu_custom_call" | custom-call | flops 6710886400 | bytes 1638400 | tf_op jit(solution)/shard_map/pallas_call | solution.py:406
  122.5 1.6 %rsqrt_multiply_fusion = f32[640,640]{1,0:T(8,128)} fusion(f32[640,640]{1,0:T(8,128)S(1)} %get-tuple-element.7, f32[640]{0:T(1024)S(1)} %get-tuple-element.10, f32[640]{0:T(1024)S(1)} %divide_subtract_fusion, f32[]{:T(128)} %bitcast, f32[640]{0:T(1024)S(1)} %get-tuple-element.9, f32[640]{0:T(1024)S(1)} %get-tuple-element.12), kind=kLoop, calls=%fused_computation | loop fusion | flops 2048000 | bytes 3287044 | tf_op jit(solution)/shard_map/div | solution.py:450
  (2 shorter events, 0.0 us)
Async XLA Ops:
  0.7 1.1 copy-start
  1.7 1.1 copy-start.1

commit v5 on v4

--- a/solution.py
+++ b/solution.py
@@ -11,25 +11,25 @@
 STRIPS = len(BOUNDS) - 1
 CUT = 32
 (
-    SPREAD, ROLL, RING_START, SWAP, RING, ARRIVE_OWN, ARRIVE_NEAR, ARRIVE_X, LATE, MULTIPLY, GIVE, RSTAT, FSTAT, HAND_ON, SHARE, FINISH, TAKE,
-) = range(17)
+    SPREAD, RING_START, SWAP, ARRIVE_OWN, RING, ARRIVE_NEAR, ARRIVE_X, LATE, MULTIPLY, GIVE, FSTAT, RSTAT, HAND_ON, SHARE, TAKE, FINISH,
+) = range(16)
 SCHEDULE = (
-    (SPREAD,), (ROLL,), (RING_START, 0), (RING_START, 1), (SWAP, 1), (SWAP, 0), (SWAP, 3), (RING, 1, 0, 1), (SWAP, 2),
-    (ARRIVE_OWN, 0), (ARRIVE_OWN, 1), (ARRIVE_OWN, 2), (RING, 1, 0, 2), (ARRIVE_NEAR, 0), (ARRIVE_NEAR, 1),
-    (RING_START, 2), (ARRIVE_X, 0, 2), (ARRIVE_NEAR, 2), (ARRIVE_X, 0, 1), (RING, 1, 1, 1), (RING, 0, 0, 1),
-    (RING, 0, 0, 2), (LATE, 0), (ARRIVE_X, 2, 1), (RING, 0, 2, 1), (ARRIVE_OWN, 3), (RING, 1, 1, 2), (ARRIVE_X, 1, 2),
-    (RING, 1, 0, 3), (ARRIVE_X, 0, 3), (RING, 1, 2, 1), (ARRIVE_X, 2, 2), (RING, 0, 1, 1), (ARRIVE_NEAR, 3),
-    (RING, 0, 0, 3), (RING, 1, 2, 2), (RING, 1, 1, 3), (ARRIVE_X, 3, 2), (ARRIVE_X, 3, 1), (ARRIVE_X, 2, 3),
-    (ARRIVE_X, 1, 1), (LATE, 1), (RING, 1, 2, 3), (ARRIVE_X, 1, 3), (LATE, 2), (RING, 0, 1, 2), (RING_START, 3),
-    (RING, 0, 0, 4), (ARRIVE_X, 3, 3), (ARRIVE_X, 4, 1), (RING, 0, 1, 3), (RING, 0, 2, 2), (RING, 1, 1, 4),
-    (RING, 1, 3, 1), (ARRIVE_X, 4, 2), (LATE, 3), (MULTIPLY, 0, 0, 4, 4), (MULTIPLY, 0, 0, 1, 1), (RING, 0, 3, 1),
-    (MULTIPLY, 0, 0, 2, 3), (RING, 1, 3, 2), (ARRIVE_X, 6, 2), (GIVE, 1), (GIVE, 0), (MULTIPLY, 1, 0, 1, 1),
-    (RSTAT, 0), (ARRIVE_X, 4, 3), (ARRIVE_X, 5, 2), (ARRIVE_X, 6, 1), (RING, 0, 3, 2), (ARRIVE_X, 7, 2), (FSTAT, 0),
-    (RING, 0, 2, 3), (RING, 1, 3, 3), (HAND_ON, 0), (ARRIVE_X, 6, 3), (HAND_ON, 1), (ARRIVE_X, 5, 1), (RING, 0, 3, 3),
-    (ARRIVE_X, 7, 1), (RING, 1, 3, 4), (MULTIPLY, 1, 0, 3, 3), (ARRIVE_X, 7, 3), (ARRIVE_X, 5, 3), (RING, 0, 2, 4),
-    (MULTIPLY, 1, 0, 2, 2), (MULTIPLY, 1, 0, 4, 4), (GIVE, 2), (GIVE, 3), (RSTAT, 1), (FSTAT, 1),
-    (MULTIPLY, 0, 1, 1, 4), (SHARE,), (HAND_ON, 3), (HAND_ON, 2), (MULTIPLY, 1, 1, 1, 4), (FINISH, 0), (FINISH, 1),
-    (FINISH, 3), (TAKE,), (FINISH, 2),
+    (SPREAD,), (RING_START, 0), (RING_START, 1), (SWAP, 1), (SWAP, 3), (SWAP, 0), (ARRIVE_OWN, 0), (RING, 1, 0, 1),
+    (ARRIVE_OWN, 1), (RING, 1, 1, 1), (SWAP, 2), (ARRIVE_OWN, 2), (ARRIVE_NEAR, 0), (ARRIVE_NEAR, 1), (RING_START, 2),
+    (RING, 1, 0, 2), (RING, 0, 0, 1), (ARRIVE_NEAR, 2), (ARRIVE_X, 0, 1), (ARRIVE_X, 0, 2), (LATE, 0),
+    (RING, 1, 2, 1), (RING, 1, 1, 2), (ARRIVE_X, 2, 1), (RING, 0, 2, 1), (RING, 0, 0, 2), (ARRIVE_OWN, 3),
+    (ARRIVE_X, 1, 2), (ARRIVE_X, 2, 2), (ARRIVE_X, 0, 3), (RING, 1, 0, 3), (RING, 0, 1, 1), (ARRIVE_NEAR, 3),
+    (RING, 1, 2, 2), (RING, 1, 1, 3), (RING, 0, 0, 3), (ARRIVE_X, 3, 2), (LATE, 2), (ARRIVE_X, 3, 1),
+    (ARRIVE_X, 2, 3), (ARRIVE_X, 1, 1), (RING, 1, 2, 3), (ARRIVE_X, 1, 3), (RING, 0, 1, 2), (RING_START, 3),
+    (ARRIVE_X, 3, 3), (RING, 0, 2, 2), (RING, 1, 1, 4), (LATE, 1), (RING, 0, 1, 3), (ARRIVE_X, 4, 1), (RING, 1, 3, 1),
+    (LATE, 3), (RING, 0, 0, 4), (ARRIVE_X, 4, 2), (MULTIPLY, 0, 0, 4, 4), (MULTIPLY, 0, 0, 1, 1), (RING, 0, 3, 1),
+    (MULTIPLY, 0, 0, 2, 3), (RING, 1, 3, 2), (GIVE, 0), (ARRIVE_X, 6, 2), (GIVE, 1), (MULTIPLY, 1, 0, 1, 1),
+    (ARRIVE_X, 5, 2), (ARRIVE_X, 6, 1), (RING, 0, 3, 2), (ARRIVE_X, 7, 2), (RING, 0, 2, 3), (ARRIVE_X, 4, 3),
+    (RING, 1, 3, 3), (FSTAT, 0), (ARRIVE_X, 6, 3), (RSTAT, 0), (HAND_ON, 0), (ARRIVE_X, 7, 3), (HAND_ON, 1),
+    (RING, 0, 3, 3), (ARRIVE_X, 7, 1), (ARRIVE_X, 5, 1), (RING, 1, 3, 4), (ARRIVE_X, 5, 3), (MULTIPLY, 1, 0, 2, 3),
+    (RING, 0, 2, 4), (MULTIPLY, 1, 0, 4, 4), (MULTIPLY, 0, 1, 1, 2), (GIVE, 2), (RSTAT, 1), (GIVE, 3), (FSTAT, 1),
+    (SHARE,), (MULTIPLY, 0, 1, 3, 4), (HAND_ON, 3), (HAND_ON, 2), (MULTIPLY, 1, 1, 1, 4), (TAKE,), (FINISH, 1),
+    (FINISH, 0), (FINISH, 3), (FINISH, 2),
 )
 
 
@@ -109,8 +109,6 @@
     def _():
         greet(swap_dev(0))
 
-    pl.semaphore_wait(barrier, len(partners) + jnp.where(crossed, 1, 0))
-
     def part(ref, i):
         return ref.at[pl.ds(pl.multiple_of(i * piece, piece), piece), :]
 
@@ -372,7 +370,7 @@
             steps[kind](*at)
 
     steps = {
-        SPREAD: spread, ROLL: roll, SWAP: swap, RING_START: ring_start, RING: ring_arrive,
+        SPREAD: spread, SWAP: swap, RING_START: ring_start, RING: ring_arrive,
         ARRIVE_OWN: arrive_own, ARRIVE_NEAR: arrive_near, LATE: late, ARRIVE_X: arrive_x, FSTAT: flow_stats, RSTAT: rain_stats,
         GIVE: give, HAND_ON: hand_on, SHARE: share_stats, FINISH: finish, TAKE: take_stats,
     }
@@ -390,6 +388,8 @@
 
     rain_part[...] = jnp.zeros(rain_part.shape, jnp.float32)
     flow_part[...] = jnp.zeros(flow_part.shape, jnp.float32)
+    roll()
+    pl.semaphore_wait(barrier, len(partners) + jnp.where(crossed, 1, 0))
     for item in SCHEDULE:
         if item[0] in (TAKE, FINISH) and once(FINISH):
             drain_edges()

time: 124 us -> 127 us (1.024)
  the two profiles are of different devices: /device:TPU:64 before, /device:TPU:104 now
where the time goes in v5:
time: 127 us; the launch traced here: 126 us
  Pallas kernels  122 us (96%)
  local copies, waits for them, and re-layouts  2.17 us (2%)
  other arithmetic  1.61 us (1%)
    pallas_call x1, Pallas kernels, local(): pl.pallas_call(kernel, out_shape=(jax.ShapeDtypeStruct((rows, rows), f32)...  122 us

profile of v5, /device:TPU:104, one launch (start us, length us, event | category | flops | bytes accessed | tf_op | source)
XLA Modules:
  0.0 126.0 jit_solution(14610770820395738623)
XLA Ops:
  0.7 0.0 copy-start
  0.7 1.1 copy-done
  1.7 0.0 copy-start.1
  1.7 1.1 copy-done.1
  2.8 121.5 %shard_map.37 = (f32[640,640]{1,0:T(8,128)S(1)}, f32[8,640]{1,0:T(8,128)S(1)}) custom-call(s32[1]{0:T(128)S(6)} %copy.4.lag_ref, bf16[640,512]{1,0:T(8,128)(2,1)S(1)} %copy-done, bf16[640,512]{1,0:T(8,128)(2,1)S(1)} %copy-done.1), custom_call_target="tpu_custom_call" | custom-call | flops 6710886400 | bytes 1638400 | tf_op jit(solution)/shard_map/pallas_call | solution.py:406
  124.4 1.6 %rsqrt_multiply_fusion = f32[640,640]{1,0:T(8,128)} fusion(f32[640,640]{1,0:T(8,128)S(1)} %get-tuple-element.7, f32[640]{0:T(1024)S(1)} %get-tuple-element.10, f32[640]{0:T(1024)S(1)} %divide_subtract_fusion, f32[]{:T(128)} %bitcast, f32[640]{0:T(1024)S(1)} %get-tuple-element.9, f32[640]{0:T(1024)S(1)} %get-tuple-element.12), kind=kLoop, calls=%fused_computation | loop fusion | flops 2048000 | bytes 3287044 | tf_op jit(solution)/shard_map/div | solution.py:450
  (2 shorter events, 0.0 us)
Async XLA Ops:
  0.7 1.1 copy-start
  1.7 1.1 copy-start.1

commit v6 on v5

--- a/solution.py
+++ b/solution.py
@@ -11,25 +11,25 @@
 STRIPS = len(BOUNDS) - 1
 CUT = 32
 (
-    SPREAD, RING_START, SWAP, ARRIVE_OWN, RING, ARRIVE_NEAR, ARRIVE_X, LATE, MULTIPLY, GIVE, FSTAT, RSTAT, HAND_ON, SHARE, TAKE, FINISH,
+    SPREAD, RING_START, SWAP, RING, ARRIVE_OWN, ARRIVE_NEAR, ARRIVE_X, LATE, MULTIPLY, GIVE, FSTAT, RSTAT, HAND_ON, SHARE, FINISH, TAKE,
 ) = range(16)
 SCHEDULE = (
-    (SPREAD,), (RING_START, 0), (RING_START, 1), (SWAP, 1), (SWAP, 3), (SWAP, 0), (ARRIVE_OWN, 0), (RING, 1, 0, 1),
-    (ARRIVE_OWN, 1), (RING, 1, 1, 1), (SWAP, 2), (ARRIVE_OWN, 2), (ARRIVE_NEAR, 0), (ARRIVE_NEAR, 1), (RING_START, 2),
-    (RING, 1, 0, 2), (RING, 0, 0, 1), (ARRIVE_NEAR, 2), (ARRIVE_X, 0, 1), (ARRIVE_X, 0, 2), (LATE, 0),
-    (RING, 1, 2, 1), (RING, 1, 1, 2), (ARRIVE_X, 2, 1), (RING, 0, 2, 1), (RING, 0, 0, 2), (ARRIVE_OWN, 3),
-    (ARRIVE_X, 1, 2), (ARRIVE_X, 2, 2), (ARRIVE_X, 0, 3), (RING, 1, 0, 3), (RING, 0, 1, 1), (ARRIVE_NEAR, 3),
-    (RING, 1, 2, 2), (RING, 1, 1, 3), (RING, 0, 0, 3), (ARRIVE_X, 3, 2), (LATE, 2), (ARRIVE_X, 3, 1),
+    (SPREAD,), (RING_START, 0), (RING_START, 1), (SWAP, 1), (SWAP, 0), (SWAP, 3), (RING, 1, 0, 1), (SWAP, 2),
+    (ARRIVE_OWN, 0), (ARRIVE_OWN, 1), (ARRIVE_OWN, 2), (RING, 1, 0, 2), (RING, 0, 0, 1), (ARRIVE_NEAR, 0),
+    (ARRIVE_NEAR, 1), (RING_START, 2), (ARRIVE_X, 0, 2), (ARRIVE_NEAR, 2), (ARRIVE_X, 0, 1), (RING, 1, 1, 1),
+    (RING, 0, 0, 2), (LATE, 0), (ARRIVE_X, 2, 1), (RING, 0, 2, 1), (ARRIVE_OWN, 3), (RING, 1, 1, 2), (ARRIVE_X, 1, 2),
+    (RING, 1, 0, 3), (RING, 1, 2, 1), (ARRIVE_X, 2, 2), (RING, 0, 1, 1), (ARRIVE_X, 0, 3), (ARRIVE_NEAR, 3),
+    (RING, 0, 0, 3), (RING, 1, 2, 2), (RING, 1, 1, 3), (ARRIVE_X, 3, 2), (LATE, 2), (ARRIVE_X, 3, 1),
     (ARRIVE_X, 2, 3), (ARRIVE_X, 1, 1), (RING, 1, 2, 3), (ARRIVE_X, 1, 3), (RING, 0, 1, 2), (RING_START, 3),
-    (ARRIVE_X, 3, 3), (RING, 0, 2, 2), (RING, 1, 1, 4), (LATE, 1), (RING, 0, 1, 3), (ARRIVE_X, 4, 1), (RING, 1, 3, 1),
-    (LATE, 3), (RING, 0, 0, 4), (ARRIVE_X, 4, 2), (MULTIPLY, 0, 0, 4, 4), (MULTIPLY, 0, 0, 1, 1), (RING, 0, 3, 1),
-    (MULTIPLY, 0, 0, 2, 3), (RING, 1, 3, 2), (GIVE, 0), (ARRIVE_X, 6, 2), (GIVE, 1), (MULTIPLY, 1, 0, 1, 1),
+    (ARRIVE_X, 3, 3), (RING, 0, 1, 3), (RING, 0, 2, 2), (RING, 1, 1, 4), (LATE, 1), (ARRIVE_X, 4, 1), (RING, 1, 3, 1),
+    (ARRIVE_X, 4, 2), (RING, 0, 0, 4), (LATE, 3), (MULTIPLY, 0, 0, 4, 4), (MULTIPLY, 0, 0, 1, 1), (RING, 0, 3, 1),
+    (MULTIPLY, 0, 0, 2, 3), (RING, 1, 3, 2), (ARRIVE_X, 6, 2), (GIVE, 1), (GIVE, 0), (MULTIPLY, 1, 0, 1, 1),
     (ARRIVE_X, 5, 2), (ARRIVE_X, 6, 1), (RING, 0, 3, 2), (ARRIVE_X, 7, 2), (RING, 0, 2, 3), (ARRIVE_X, 4, 3),
-    (RING, 1, 3, 3), (FSTAT, 0), (ARRIVE_X, 6, 3), (RSTAT, 0), (HAND_ON, 0), (ARRIVE_X, 7, 3), (HAND_ON, 1),
-    (RING, 0, 3, 3), (ARRIVE_X, 7, 1), (ARRIVE_X, 5, 1), (RING, 1, 3, 4), (ARRIVE_X, 5, 3), (MULTIPLY, 1, 0, 2, 3),
-    (RING, 0, 2, 4), (MULTIPLY, 1, 0, 4, 4), (MULTIPLY, 0, 1, 1, 2), (GIVE, 2), (RSTAT, 1), (GIVE, 3), (FSTAT, 1),
-    (SHARE,), (MULTIPLY, 0, 1, 3, 4), (HAND_ON, 3), (HAND_ON, 2), (MULTIPLY, 1, 1, 1, 4), (TAKE,), (FINISH, 1),
-    (FINISH, 0), (FINISH, 3), (FINISH, 2),
+    (FSTAT, 0), (RING, 1, 3, 3), (ARRIVE_X, 6, 3), (RSTAT, 0), (HAND_ON, 0), (ARRIVE_X, 7, 3), (ARRIVE_X, 5, 3),
+    (RING, 0, 3, 3), (HAND_ON, 1), (ARRIVE_X, 7, 1), (ARRIVE_X, 5, 1), (RING, 1, 3, 4), (MULTIPLY, 1, 0, 2, 3),
+    (RING, 0, 2, 4), (MULTIPLY, 1, 0, 4, 4), (GIVE, 2), (RSTAT, 1), (GIVE, 3), (FSTAT, 1), (MULTIPLY, 0, 1, 1, 4),
+    (SHARE,), (HAND_ON, 3), (HAND_ON, 2), (FINISH, 1), (FINISH, 0), (MULTIPLY, 1, 1, 1, 4), (TAKE,), (FINISH, 2),
+    (FINISH, 3),
 )
 
 
@@ -251,19 +251,21 @@
         if start:
             acc[h, at, :] = jnp.zeros((hi - lo, rows), jnp.float32)
 
-        def step(i, carry):
-            s = low + lax.div(i, 2)
-            zd = zo_(jnp.where(lax.rem(i, 2) == 0, s, 1 - s))
-            before = rain_all[zd, at, 0:LANES].astype(jnp.float32)
-            here = rain_all[zd + 1, at, 0:LANES].astype(jnp.float32)
-            head = jnp.where(lane < lag, before, here).astype(jnp.bfloat16)
-            used = jnp.concatenate([head, rain_all[zd + 1, at, LANES:]], axis=1)
+        def step(s, carry):
+            used, cells = [], []
+            for zd in (zo_(s), zo_(1 - s)):
+                before = rain_all[zd, at, 0:LANES].astype(jnp.float32)
+                here = rain_all[zd + 1, at, 0:LANES].astype(jnp.float32)
+                head = jnp.where(lane < lag, before, here).astype(jnp.bfloat16)
+                used.append(jnp.concatenate([head, rain_all[zd + 1, at, LANES:]], axis=1))
+                cells.append(flow_all[lax.rem(zd, 2), lax.div(zd, 2), half])
             acc[h, at, :] += lax.dot_general(
-                used, flow_all[lax.rem(zd, 2), lax.div(zd, 2), half], (((1,), (1,)), ((), ())), preferred_element_type=jnp.float32
+                jnp.concatenate(used, axis=1), jnp.concatenate(cells, axis=1),
+                (((1,), (1,)), ((), ())), preferred_element_type=jnp.float32,
             )
             return carry
 
-        lax.fori_loop(0, 2 * (high - low + 1), step, 0)
+        lax.fori_loop(low, high + 1, step, 0)
 
     def rain_stats(w):
         lo, hi = BOUNDS[2 * w], BOUNDS[2 * w + 2]

time: 127 us -> 122 us (0.961)
  Pallas kernels: 122 us -> 118 us
    pallas_call x1, Pallas kernels: 122 us -> 118 us  [local(): pl.pallas_call(kernel, out_shape=(jax.ShapeDtypeStruct((rows, rows), f32)...]
where the time goes in v6:
time: 122 us
  Pallas kernels  118 us (97%)
  local copies, waits for them, and re-layouts  2.17 us (2%)
  other arithmetic  1.61 us (1%)
    pallas_call x1, Pallas kernels, local(): pl.pallas_call(kernel, out_shape=(jax.ShapeDtypeStruct((rows, rows), f32)...  118 us

profile of v6, /device:TPU:104, one launch (start us, length us, event | category | flops | bytes accessed | tf_op | source)
XLA Modules:
  0.0 122.1 jit_solution(7867198836894418)
XLA Ops:
  0.7 0.0 copy-start
  0.7 1.1 copy-done
  1.7 0.0 copy-start.1
  1.7 1.1 copy-done.1
  2.8 117.7 %shard_map.37 = (f32[640,640]{1,0:T(8,128)S(1)}, f32[8,640]{1,0:T(8,128)S(1)}) custom-call(s32[1]{0:T(128)S(6)} %copy.4.lag_ref, bf16[640,512]{1,0:T(8,128)(2,1)S(1)} %copy-done, bf16[640,512]{1,0:T(8,128)(2,1)S(1)} %copy-done.1), custom_call_target="tpu_custom_call" | custom-call | flops 6710886400 | bytes 1638400 | tf_op jit(solution)/shard_map/pallas_call | solution.py:408
  120.6 1.6 %rsqrt_multiply_fusion = f32[640,640]{1,0:T(8,128)} fusion(f32[640,640]{1,0:T(8,128)S(1)} %get-tuple-element.7, f32[640]{0:T(1024)S(1)} %get-tuple-element.10, f32[640]{0:T(1024)S(1)} %divide_subtract_fusion, f32[]{:T(128)} %bitcast, f32[640]{0:T(1024)S(1)} %get-tuple-element.9, f32[640]{0:T(1024)S(1)} %get-tuple-element.12), kind=kLoop, calls=%fused_computation | loop fusion | flops 2048000 | bytes 3287044 | tf_op jit(solution)/shard_map/div | solution.py:452
  (2 shorter events, 0.0 us)
Async XLA Ops:
  0.7 1.1 copy-start
  1.7 1.1 copy-start.1

commit v7 on v6

--- a/solution.py
+++ b/solution.py
@@ -11,25 +11,25 @@
 STRIPS = len(BOUNDS) - 1
 CUT = 32
 (
-    SPREAD, RING_START, SWAP, RING, ARRIVE_OWN, ARRIVE_NEAR, ARRIVE_X, LATE, MULTIPLY, GIVE, FSTAT, RSTAT, HAND_ON, SHARE, FINISH, TAKE,
+    SPREAD, RING_START, SWAP, ARRIVE_OWN, RING, ARRIVE_NEAR, ARRIVE_X, LATE, MULTIPLY, GIVE, RSTAT, FSTAT, HAND_ON, SHARE, TAKE, FINISH,
 ) = range(16)
 SCHEDULE = (
-    (SPREAD,), (RING_START, 0), (RING_START, 1), (SWAP, 1), (SWAP, 0), (SWAP, 3), (RING, 1, 0, 1), (SWAP, 2),
-    (ARRIVE_OWN, 0), (ARRIVE_OWN, 1), (ARRIVE_OWN, 2), (RING, 1, 0, 2), (RING, 0, 0, 1), (ARRIVE_NEAR, 0),
-    (ARRIVE_NEAR, 1), (RING_START, 2), (ARRIVE_X, 0, 2), (ARRIVE_NEAR, 2), (ARRIVE_X, 0, 1), (RING, 1, 1, 1),
-    (RING, 0, 0, 2), (LATE, 0), (ARRIVE_X, 2, 1), (RING, 0, 2, 1), (ARRIVE_OWN, 3), (RING, 1, 1, 2), (ARRIVE_X, 1, 2),
-    (RING, 1, 0, 3), (RING, 1, 2, 1), (ARRIVE_X, 2, 2), (RING, 0, 1, 1), (ARRIVE_X, 0, 3), (ARRIVE_NEAR, 3),
-    (RING, 0, 0, 3), (RING, 1, 2, 2), (RING, 1, 1, 3), (ARRIVE_X, 3, 2), (LATE, 2), (ARRIVE_X, 3, 1),
-    (ARRIVE_X, 2, 3), (ARRIVE_X, 1, 1), (RING, 1, 2, 3), (ARRIVE_X, 1, 3), (RING, 0, 1, 2), (RING_START, 3),
-    (ARRIVE_X, 3, 3), (RING, 0, 1, 3), (RING, 0, 2, 2), (RING, 1, 1, 4), (LATE, 1), (ARRIVE_X, 4, 1), (RING, 1, 3, 1),
-    (ARRIVE_X, 4, 2), (RING, 0, 0, 4), (LATE, 3), (MULTIPLY, 0, 0, 4, 4), (MULTIPLY, 0, 0, 1, 1), (RING, 0, 3, 1),
-    (MULTIPLY, 0, 0, 2, 3), (RING, 1, 3, 2), (ARRIVE_X, 6, 2), (GIVE, 1), (GIVE, 0), (MULTIPLY, 1, 0, 1, 1),
-    (ARRIVE_X, 5, 2), (ARRIVE_X, 6, 1), (RING, 0, 3, 2), (ARRIVE_X, 7, 2), (RING, 0, 2, 3), (ARRIVE_X, 4, 3),
-    (FSTAT, 0), (RING, 1, 3, 3), (ARRIVE_X, 6, 3), (RSTAT, 0), (HAND_ON, 0), (ARRIVE_X, 7, 3), (ARRIVE_X, 5, 3),
-    (RING, 0, 3, 3), (HAND_ON, 1), (ARRIVE_X, 7, 1), (ARRIVE_X, 5, 1), (RING, 1, 3, 4), (MULTIPLY, 1, 0, 2, 3),
-    (RING, 0, 2, 4), (MULTIPLY, 1, 0, 4, 4), (GIVE, 2), (RSTAT, 1), (GIVE, 3), (FSTAT, 1), (MULTIPLY, 0, 1, 1, 4),
-    (SHARE,), (HAND_ON, 3), (HAND_ON, 2), (FINISH, 1), (FINISH, 0), (MULTIPLY, 1, 1, 1, 4), (TAKE,), (FINISH, 2),
-    (FINISH, 3),
+    (SPREAD,), (RING_START, 0), (RING_START, 1), (SWAP, 1), (SWAP, 0), (SWAP, 3), (ARRIVE_OWN, 0), (RING, 1, 0, 1),
+    (ARRIVE_OWN, 1), (SWAP, 2), (ARRIVE_OWN, 2), (RING, 1, 0, 2), (RING, 0, 0, 1), (ARRIVE_NEAR, 0), (ARRIVE_NEAR, 1),
+    (RING_START, 2), (ARRIVE_X, 0, 2), (ARRIVE_NEAR, 2), (ARRIVE_X, 0, 1), (RING, 1, 1, 1), (RING, 0, 0, 2),
+    (LATE, 0), (ARRIVE_OWN, 3), (ARRIVE_X, 2, 1), (RING, 1, 1, 2), (ARRIVE_X, 1, 2), (RING, 1, 0, 3),
+    (ARRIVE_X, 2, 2), (RING, 0, 1, 1), (RING, 0, 2, 1), (ARRIVE_X, 0, 3), (RING, 1, 2, 1), (RING, 0, 0, 3),
+    (ARRIVE_NEAR, 3), (RING, 1, 1, 3), (ARRIVE_X, 3, 2), (LATE, 2), (RING, 1, 2, 2), (ARRIVE_X, 3, 1),
+    (ARRIVE_X, 2, 3), (ARRIVE_X, 1, 1), (ARRIVE_X, 1, 3), (RING, 0, 1, 2), (RING_START, 3), (ARRIVE_X, 3, 3),
+    (RING, 0, 1, 3), (RING, 0, 0, 4), (RING, 1, 2, 3), (RING, 1, 1, 4), (RING, 0, 2, 2), (ARRIVE_X, 4, 1), (LATE, 1),
+    (MULTIPLY, 0, 0, 4, 4), (ARRIVE_X, 4, 2), (RING, 1, 3, 1), (LATE, 3), (MULTIPLY, 0, 0, 1, 1), (RING, 0, 3, 1),
+    (MULTIPLY, 0, 0, 2, 3), (RING, 1, 3, 2), (GIVE, 1), (GIVE, 0), (ARRIVE_X, 5, 2), (MULTIPLY, 1, 0, 1, 1),
+    (RING, 0, 3, 2), (ARRIVE_X, 6, 1), (ARRIVE_X, 6, 2), (RING, 0, 2, 3), (RSTAT, 0), (ARRIVE_X, 7, 2),
+    (RING, 1, 3, 3), (ARRIVE_X, 4, 3), (FSTAT, 0), (ARRIVE_X, 6, 3), (RING, 0, 3, 3), (ARRIVE_X, 7, 3),
+    (RING, 1, 3, 4), (ARRIVE_X, 5, 3), (HAND_ON, 0), (RING, 0, 2, 4), (HAND_ON, 1), (ARRIVE_X, 7, 1),
+    (ARRIVE_X, 5, 1), (MULTIPLY, 1, 0, 2, 4), (GIVE, 2), (FSTAT, 1), (RSTAT, 1), (GIVE, 3), (SHARE,),
+    (MULTIPLY, 0, 1, 1, 4), (HAND_ON, 2), (HAND_ON, 3), (MULTIPLY, 1, 1, 1, 4), (TAKE,), (FINISH, 0), (FINISH, 1),
+    (FINISH, 2), (FINISH, 3),
 )
 
 

time: 122 us -> 125 us (1.025); the launches traced: 122 us -> 124 us
    pallas_call x1, Pallas kernels: 118 us -> 119 us  [local(): pl.pallas_call(kernel, out_shape=(jax.ShapeDtypeStruct((rows, rows), f32)...]
where the time goes in v7:
time: 125 us; the launch traced here: 124 us
  Pallas kernels  119 us (95%)
  local copies, waits for them, and re-layouts  2.17 us (2%)
  other arithmetic  1.61 us (1%)
    pallas_call x1, Pallas kernels, local(): pl.pallas_call(kernel, out_shape=(jax.ShapeDtypeStruct((rows, rows), f32)...  119 us

profile of v7, /device:TPU:104, one launch (start us, length us, event | category | flops | bytes accessed | tf_op | source)
XLA Modules:
  0.0 123.7 jit_solution(11361845522988231734)
XLA Ops:
  0.7 0.0 copy-start
  0.7 1.1 copy-done
  1.7 0.0 copy-start.1
  1.7 1.1 copy-done.1
  2.8 119.3 %shard_map.37 = (f32[640,640]{1,0:T(8,128)S(1)}, f32[8,640]{1,0:T(8,128)S(1)}) custom-call(s32[1]{0:T(128)S(6)} %copy.4.lag_ref, bf16[640,512]{1,0:T(8,128)(2,1)S(1)} %copy-done, bf16[640,512]{1,0:T(8,128)(2,1)S(1)} %copy-done.1), custom_call_target="tpu_custom_call" | custom-call | flops 6710886400 | bytes 1638400 | tf_op jit(solution)/shard_map/pallas_call | solution.py:408
  122.2 1.6 %rsqrt_multiply_fusion = f32[640,640]{1,0:T(8,128)} fusion(f32[640,640]{1,0:T(8,128)S(1)} %get-tuple-element.7, f32[640]{0:T(1024)S(1)} %get-tuple-element.10, f32[640]{0:T(1024)S(1)} %divide_subtract_fusion, f32[]{:T(128)} %bitcast, f32[640]{0:T(1024)S(1)} %get-tuple-element.9, f32[640]{0:T(1024)S(1)} %get-tuple-element.12), kind=kLoop, calls=%fused_computation | loop fusion | flops 2048000 | bytes 3287044 | tf_op jit(solution)/shard_map/div | solution.py:452
  (2 shorter events, 0.0 us)
Async XLA Ops:
  0.7 1.1 copy-start
  1.7 1.1 copy-start.1
